TPU v7x, 128 devices: a whole 4x4x4 slice. The times are simulated.
128 devices in a mesh: dp: 8 (over z, x_lo), ctx: 16 (over y, x_hi, core).
Axes of the slice: x: 4 (x_hi: 2, x_lo: 2; x = x_hi * 2 + x_lo), y: 4, z: 4, core: 2. Of those that a mesh axis runs over, the one named last changes fastest.
Arguments:
- hidden_in: bfloat16 [8, 2048, 512], P('dp', 'ctx'), may hold values from -6 to 6
- positions: int32 [8, 2048], P('dp', 'ctx'), may hold values from 0 to 127, as said below
- block_order: int32 [32], replicated, may hold values from 0 to 31, as said below
- norm1_gain: bfloat16 [512], P(('dp', 'ctx')), may hold values from 0.5 to 1.5
- norm1_bias: bfloat16 [512], P(('dp', 'ctx')), may hold values from -1 to 1
- norm2_gain: bfloat16 [512], P(('dp', 'ctx')), may hold values from 0.5 to 1.5
- norm2_bias: bfloat16 [512], P(('dp', 'ctx')), may hold values from -1 to 1
- qkv_weight: bfloat16 [512, 1536], P(('dp', 'ctx')), may hold values from -0.25 to 0.25
- qkv_bias: bfloat16 [1536], P(('dp', 'ctx')), may hold values from -1.5 to 1.5
- attn_out_weight: bfloat16 [512, 512], P(('dp', 'ctx')), may hold values from -1 to 1
- out_bias: bfloat16 [512], P(('dp', 'ctx')), may hold values from -1.5 to 1.5
- up_weight: bfloat16 [512, 2048], P(('dp', 'ctx')), may hold values from -0.25 to 0.25
- up_bias: bfloat16 [2048], P(('dp', 'ctx')), may hold values from -1.5 to 1.5
- down_weight: bfloat16 [2048, 512], P(('dp', 'ctx')), may hold values from -0.125 to 0.125
- out_grad: bfloat16 [8, 2048, 512], P('dp', 'ctx'), may hold values from -6 to 6
Outputs:
- block_out: bfloat16 [8, 2048, 512], P('dp', 'ctx')
- input_grad: float32 [8, 2048, 512], P('dp', 'ctx')
- norm1_gain_grad: float32 [512], P(('dp', 'ctx'))
- norm1_bias_grad: float32 [512], P(('dp', 'ctx'))
- norm2_gain_grad: float32 [512], P(('dp', 'ctx'))
- norm2_bias_grad: float32 [512], P(('dp', 'ctx'))
- qkv_weight_grad: float32 [512, 1536], P(('dp', 'ctx'))
- qk_bias_grad: float32 [1024], P(('dp', 'ctx'))
- value_bias_grad: float32 [512], P(('dp', 'ctx'))
- attn_out_weight_grad: float32 [512, 512], P(('dp', 'ctx'))
- out_bias_grad: float32 [512], P(('dp', 'ctx'))
- up_weight_grad: float32 [512, 2048], P(('dp', 'ctx'))
- up_bias_grad: float32 [2048], P(('dp', 'ctx'))
- down_weight_grad: float32 [2048, 512], P(('dp', 'ctx'))
Inputs may be any that keep to these rules, and one draw needn't show every extreme that they name: `block_order`: slots 2c and 2c+1 hold blocks j and 31 - j for some j; every block appears once. `positions`: positions count up by one along a sequence's true order and restart at 0 at the start of each packed document; a document starts at every multiple of 128 true rows and possibly in between; the first document of each sequence has exactly 128 rows.
All inputs are finite; a program needn't handle non-finite values.
Results may differ from a plain program's by a relative error of at most 0.025.
Values may be sent and summed in bfloat16 or wider, within the bound.
A program may use at most 128 MiB of HBM per device.

v0:
```python
import jax
import jax.numpy as jnp
from jax import lax
from jax.sharding import PartitionSpec as P

HEAD_DIM = 64
ROT_DIM = 16


EPS = 1e-05
NEG_BIG = -1e30


def layer_norm(values, gain, shift):
    center = values - jnp.mean(values, axis=-1, keepdims=True)
    spread = jnp.mean(center * center, axis=-1, keepdims=True)
    return center * lax.rsqrt(spread + EPS) * gain + shift


def rotary(tensor, places):
    half_rot = ROT_DIM // 2
    freqs = 10000.0 ** (-jnp.arange(half_rot, dtype=jnp.float32) * 2.0 / ROT_DIM)
    angle = places.astype(jnp.float32)[:, None] * freqs[None, :]
    angle = jnp.concatenate([angle, angle], axis=-1)[:, None, :]
    turned_part = tensor[..., :ROT_DIM]
    swapped = jnp.concatenate([-turned_part[..., half_rot:], turned_part[..., :half_rot]], axis=-1)
    return jnp.concatenate(
        [turned_part * jnp.cos(angle) + swapped * jnp.sin(angle), tensor[..., ROT_DIM:]], axis=-1
    )


def cross_rows(left, right):
    return lax.dot_general(
        left, right, (((0,), (0,)), ((), ())), preferred_element_type=jnp.float32
    )


def against(left, right):
    return lax.dot_general(
        left, right, (((1,), (1,)), ((), ())), preferred_element_type=jnp.float32
    )


def true_rows(table, start, count, blk_rows):
    stored = start + jnp.arange(count, dtype=jnp.int32)
    slot_of = stored // blk_rows
    slot_ids = jnp.arange(table.shape[0], dtype=jnp.int32)
    chosen = jnp.sum(jnp.where(slot_of[:, None] == slot_ids[None, :], table[None, :], 0), axis=1)
    return chosen * blk_rows + stored % blk_rows


def per_device(
    hidden_in,
    positions,
    block_order,
    norm1_gain,
    norm1_bias,
    norm2_gain,
    norm2_bias,
    qkv_weight,
    qkv_bias,
    attn_out_weight,
    out_bias,
    up_weight,
    up_bias,
    down_weight,
    out_grad,
):
    gathered = (
        lax.all_gather(norm1_gain, ("dp", "ctx"), axis=0, tiled=True),
        lax.all_gather(norm1_bias, ("dp", "ctx"), axis=0, tiled=True),
        lax.all_gather(norm2_gain, ("dp", "ctx"), axis=0, tiled=True),
        lax.all_gather(norm2_bias, ("dp", "ctx"), axis=0, tiled=True),
        lax.all_gather(qkv_weight, ("dp", "ctx"), axis=0, tiled=True),
        lax.all_gather(qkv_bias, ("dp", "ctx"), axis=0, tiled=True),
        lax.all_gather(attn_out_weight, ("dp", "ctx"), axis=0, tiled=True),
        lax.all_gather(out_bias, ("dp", "ctx"), axis=0, tiled=True),
        lax.all_gather(up_weight, ("dp", "ctx"), axis=0, tiled=True),
        lax.all_gather(up_bias, ("dp", "ctx"), axis=0, tiled=True),
        lax.all_gather(down_weight, ("dp", "ctx"), axis=0, tiled=True),
    )
    gain_one, shift_one, gain_two, shift_two, w_qkv, b_qkv, w_out, b_out, w_up, b_up, w_down = (
        gathered
    )
    inputs = hidden_in[0].astype(jnp.float32)
    nrows, width = inputs.shape
    head_dim = HEAD_DIM
    heads = width // head_dim
    blk_rows = nrows // 2
    factor = head_dim ** (-0.5)
    place_ctx = lax.axis_index("ctx")
    query_true = true_rows(block_order, place_ctx * nrows, nrows, blk_rows)
    places = positions[0]

    def norms(values, g_one, s_one, g_two, s_two):
        return (layer_norm(values, g_one, s_one), layer_norm(values, g_two, s_two))

    (normed_one, normed_two), norm_pull = jax.vjp(
        norms,
        inputs,
        gain_one.astype(jnp.float32),
        shift_one.astype(jnp.float32),
        gain_two.astype(jnp.float32),
        shift_two.astype(jnp.float32),
    )
    normed_one = normed_one.astype(jnp.bfloat16)
    normed_two = normed_two.astype(jnp.bfloat16)
    qkv = (
        jnp.dot(normed_one, w_qkv, preferred_element_type=jnp.float32) + b_qkv.astype(jnp.float32)
    ).reshape(nrows, 3, heads, head_dim)

    def turn_both(q_part, k_part):
        return (rotary(q_part, places), rotary(k_part, places))

    (q_turned, k_turned), turn_pull = jax.vjp(turn_both, qkv[:, 0], qkv[:, 1])
    queries = q_turned.astype(jnp.bfloat16)
    own_keys = k_turned.reshape(nrows, width).astype(jnp.bfloat16)
    own_vals = qkv[:, 2].reshape(nrows, width).astype(jnp.bfloat16)
    all_keys, all_vals = (
        lax.all_gather(own_keys, "ctx", axis=0, tiled=True),
        lax.all_gather(own_vals, "ctx", axis=0, tiled=True),
    )
    seq_rows = all_keys.shape[0]
    key_rows = min(512, seq_rows)
    key_steps = jnp.arange(seq_rows // key_rows, dtype=jnp.int32)

    def scores_for(key_src, start):
        k_part = lax.dynamic_slice_in_dim(key_src, start, key_rows, 0).reshape(
            key_rows, heads, head_dim
        )
        scores = (
            jnp.einsum("qhd,khd->hqk", queries, k_part, preferred_element_type=jnp.float32) * factor
        )
        key_true = true_rows(block_order, start, key_rows, blk_rows)
        allowed = query_true[:, None] >= key_true[None, :]
        return (scores, allowed[None], k_part)

    def stats_step(carry, step_id):
        running_top, running_sum = carry
        scores, allowed, k_part = scores_for(all_keys, step_id * key_rows)
        new_top = jnp.maximum(running_top, jnp.max(jnp.where(allowed, scores, NEG_BIG), axis=-1))
        running_sum = running_sum * jnp.exp(running_top - new_top) + jnp.sum(
            jnp.where(allowed, jnp.exp(scores - new_top[..., None]), 0.0), axis=-1
        )
        return ((new_top, running_sum), None)

    start_top = jnp.full((heads, nrows), NEG_BIG, jnp.float32)
    (row_top, row_sum), unused = lax.scan(
        stats_step, (start_top, jnp.zeros((heads, nrows), jnp.float32)), key_steps
    )
    log_total = row_top + jnp.log(row_sum)

    def mix_step(accum, step_id):
        start = step_id * key_rows
        scores, allowed, k_part = scores_for(all_keys, start)
        probs = jnp.where(allowed, jnp.exp(scores - log_total[..., None]), 0.0).astype(jnp.bfloat16)
        v_part = lax.dynamic_slice_in_dim(all_vals, start, key_rows, 0).reshape(
            key_rows, heads, head_dim
        )
        return (
            accum + jnp.einsum("hqk,khd->qhd", probs, v_part, preferred_element_type=jnp.float32),
            None,
        )

    attended, unused = lax.scan(
        mix_step, jnp.zeros((nrows, heads, head_dim), jnp.float32), key_steps
    )
    mixed_att = attended.reshape(nrows, width).astype(jnp.bfloat16)
    upper = jnp.dot(normed_two, w_up, preferred_element_type=jnp.float32) + b_up.astype(jnp.float32)
    gelu_val, gelu_pull = jax.vjp(lambda arg_in: jax.nn.gelu(arg_in, approximate=False), upper)
    gelu_out = gelu_val.astype(jnp.bfloat16)
    result = (
        inputs
        + jnp.dot(mixed_att, w_out, preferred_element_type=jnp.float32)
        + jnp.dot(gelu_out, w_down, preferred_element_type=jnp.float32)
        + b_out.astype(jnp.float32)
    )
    block_out = result.astype(jnp.bfloat16)[None]
    back_qkv, back_out, back_up, back_down = (
        lax.all_gather(qkv_weight, ("dp", "ctx"), axis=0, tiled=True),
        lax.all_gather(attn_out_weight, ("dp", "ctx"), axis=0, tiled=True),
        lax.all_gather(up_weight, ("dp", "ctx"), axis=0, tiled=True),
        lax.all_gather(down_weight, ("dp", "ctx"), axis=0, tiled=True),
    )
    grad_out = out_grad[0]
    d_mixed = against(grad_out, back_out).astype(jnp.bfloat16)
    grad_w_out = cross_rows(mixed_att, grad_out)
    grad_w_down = cross_rows(gelu_out, grad_out)
    grad_b_out = jnp.sum(grad_out.astype(jnp.float32), axis=0)
    d_gelu = against(grad_out, back_down)
    d_upper = gelu_pull(d_gelu)[0].astype(jnp.bfloat16)
    grad_w_up = cross_rows(normed_two, d_upper)
    grad_b_up = jnp.sum(d_upper.astype(jnp.float32), axis=0)
    d_normed_two = against(d_upper, back_up)
    d_heads = d_mixed.reshape(nrows, heads, head_dim)
    delta = jnp.einsum("qhd,qhd->hq", d_heads.astype(jnp.float32), attended)
    back_keys, back_vals = (all_keys, all_vals)

    def grad_step(d_query, step_id):
        start = step_id * key_rows
        scores, allowed, k_part = scores_for(back_keys, start)
        probs = jnp.where(allowed, jnp.exp(scores - log_total[..., None]), 0.0)
        v_part = lax.dynamic_slice_in_dim(back_vals, start, key_rows, 0).reshape(
            key_rows, heads, head_dim
        )
        d_probs = jnp.einsum("qhd,khd->hqk", d_heads, v_part, preferred_element_type=jnp.float32)
        d_scores = (probs * (d_probs - delta[..., None])).astype(jnp.bfloat16)
        d_query = d_query + factor * jnp.einsum(
            "hqk,khd->qhd", d_scores, k_part, preferred_element_type=jnp.float32
        )
        d_key_part = factor * jnp.einsum(
            "hqk,qhd->khd", d_scores, queries, preferred_element_type=jnp.float32
        )
        d_val_part = jnp.einsum(
            "hqk,qhd->khd", probs.astype(jnp.bfloat16), d_heads, preferred_element_type=jnp.float32
        )
        return (d_query, (d_key_part.reshape(key_rows, width), d_val_part.reshape(key_rows, width)))

    d_query, (d_key_all, d_val_all) = lax.scan(
        grad_step, jnp.zeros((nrows, heads, head_dim), jnp.float32), key_steps
    )
    d_key_all = d_key_all.reshape(seq_rows, width)
    d_val_all = d_val_all.reshape(seq_rows, width)
    d_key_own, d_val_own = (
        lax.psum_scatter(
            d_key_all.astype(jnp.bfloat16), "ctx", scatter_dimension=0, tiled=True
        ).astype(jnp.float32),
        lax.psum_scatter(
            d_val_all.astype(jnp.bfloat16), "ctx", scatter_dimension=0, tiled=True
        ).astype(jnp.float32),
    )
    d_q_pre, d_k_pre = turn_pull((d_query, d_key_own.reshape(nrows, heads, head_dim)))
    d_qkv = (
        jnp.stack([d_q_pre, d_k_pre, d_val_own.reshape(nrows, heads, head_dim)], axis=1)
        .reshape(nrows, 3 * width)
        .astype(jnp.bfloat16)
    )
    grad_w_qkv = cross_rows(normed_one, d_qkv)
    grad_b_qkv = jnp.sum(d_qkv.astype(jnp.float32), axis=0)
    grad_b_qk = grad_b_qkv[: 2 * width]
    grad_b_val = grad_b_qkv[2 * width :]
    d_normed_one = against(d_qkv, back_qkv)
    d_inputs, grad_g_one, grad_s_one, grad_g_two, grad_s_two = norm_pull(
        (d_normed_one, d_normed_two)
    )
    input_grad = (grad_out.astype(jnp.float32) + d_inputs)[None]
    owned = (
        lax.psum_scatter(grad_g_one, ("dp", "ctx"), scatter_dimension=0, tiled=True),
        lax.psum_scatter(grad_s_one, ("dp", "ctx"), scatter_dimension=0, tiled=True),
        lax.psum_scatter(grad_g_two, ("dp", "ctx"), scatter_dimension=0, tiled=True),
        lax.psum_scatter(grad_s_two, ("dp", "ctx"), scatter_dimension=0, tiled=True),
        lax.psum_scatter(grad_w_qkv, ("dp", "ctx"), scatter_dimension=0, tiled=True),
        lax.psum_scatter(grad_b_qk, ("dp", "ctx"), scatter_dimension=0, tiled=True),
        lax.psum_scatter(grad_b_val, ("dp", "ctx"), scatter_dimension=0, tiled=True),
        lax.psum_scatter(grad_w_out, ("dp", "ctx"), scatter_dimension=0, tiled=True),
        lax.psum_scatter(grad_b_out, ("dp", "ctx"), scatter_dimension=0, tiled=True),
        lax.psum_scatter(grad_w_up, ("dp", "ctx"), scatter_dimension=0, tiled=True),
        lax.psum_scatter(grad_b_up, ("dp", "ctx"), scatter_dimension=0, tiled=True),
        lax.psum_scatter(grad_w_down, ("dp", "ctx"), scatter_dimension=0, tiled=True),
    )
    return (
        block_out,
        input_grad,
        owned[0],
        owned[1],
        owned[2],
        owned[3],
        owned[4],
        owned[5],
        owned[6],
        owned[7],
        owned[8],
        owned[9],
        owned[10],
        owned[11],
    )


def solution(mesh):
    placed = (
        P("dp", "ctx", None),
        P("dp", "ctx"),
        P(),
        P(("dp", "ctx")),
        P(("dp", "ctx")),
        P(("dp", "ctx")),
        P(("dp", "ctx")),
        P(("dp", "ctx"), None),
        P(("dp", "ctx")),
        P(("dp", "ctx"), None),
        P(("dp", "ctx")),
        P(("dp", "ctx"), None),
        P(("dp", "ctx")),
        P(("dp", "ctx"), None),
        P("dp", "ctx", None),
    )
    return jax.shard_map(
        per_device,
        mesh=mesh,
        in_specs=placed,
        out_specs=(
            P("dp", "ctx", None),
            P("dp", "ctx", None),
            P(("dp", "ctx")),
            P(("dp", "ctx")),
            P(("dp", "ctx")),
            P(("dp", "ctx")),
            P(("dp", "ctx"), None),
            P(("dp", "ctx")),
            P(("dp", "ctx")),
            P(("dp", "ctx"), None),
            P(("dp", "ctx")),
            P(("dp", "ctx"), None),
            P(("dp", "ctx")),
            P(("dp", "ctx"), None),
        ),
        check_vma=False,
    )
```

profile of v0, /device:TPU:1, one launch (start us, length us, event | category | flops | bytes accessed | tf_op | source)
XLA Modules:
  0.0 1654.1 jit_solution(12489906655974821921)
XLA Ops:
  13.9 69.1 %all-reduce.28 = (bf16[1536]{0:T(1024)(128)(2,1)S(1)}, bf16[512]{0:T(512)(128)(2,1)S(1)}, bf16[512]{0:T(512)(128)(2,1)S(1)}, bf16[2048]{0:T(1024)(128)(2,1)}, bf...) all-reduce(bf16[1536]{0:T(1024)(128)(2,1)S(1)} %dynamic-update-slic, ...), channel_id=1, replica_groups=mesh['dp'=8,'ctx'=16] {'dp','ctx'}, use_global_device_ids=true, to_apply=%add.10 | all-reduce | flops 6144 | bytes 24576
  86.0 120.2 %all-gather.15.cloned.1.call-done = bf16[128,4,1536]{2,1,0:T(4,128)(2,1)} async-done(((bf16[1,4,1536]{2,1,0:T(4,128)(2,1)}), bf16[128,4,1536]{2,1,0:T(4,128)(2,1)}) %all-gather.15.cloned.1.call-update) | async-done | bytes 1572880 | tf_op jit(solution)/shard_map/all_gather | solution.py:74
  206.2 2.7 reshape.477
  213.1 176.8 %all-gather.1 = bf16[128,4,512]{2,1,0:T(4,128)(2,1)S(1)} all-gather(bf16[1,4,512]{2,1,0:T(4,128)(2,1)S(1)} %bitcast.279), channel_id=1, replica_groups=mesh['dp'=8,'ctx'=16] {'dp','ctx'}, dimensions={0}, use_global_device_ids=true | all-gather | bytes 528384 | tf_op jit(solution)/shard_map/all_gather | solution.py:76
  391.4 14.7 while.45
  392.9 1.1 constant_dynamic-slice_fusion.12
  396.6 1.1 constant_dynamic-slice_fusion.12
  403.9 1.1 constant_dynamic-slice_fusion.12
  406.1 14.6 while.46
  407.4 1.3 constant_dynamic-slice_fusion.13
  411.0 1.3 constant_dynamic-slice_fusion.13
  414.7 1.3 constant_dynamic-slice_fusion.13
  418.3 1.3 constant_dynamic-slice_fusion.13
  421.5 45.7 %while.47 = (s32[]{:T(128)}, f32[128,8,64]{0,2,1:T(8,128)}, bf16[4,512,512]{2,1,0:T(8,128)(2,1)}, bf16[4,512,512]{2,1,0:T(8,128)(2,1)}, s32[4]{0:T(128)S(1)}, /*...) while((s32[]{:T(128)}, f32[128,8,64]{0,2,1:T(8,128)}, ...), condition=%wide.region_15.16_spmd.clone, body=%wide.region_13.15_spmd.clone.sunk | while | flops 340064768 | bytes 21681288 | solution.py:219
  424.8 1.1 constant_dynamic-slice_fusion.15
  426.4 2.1 fusion.185
  428.5 1.3 fusion.186
  429.8 1.3 copy.108
  436.1 1.1 constant_dynamic-slice_fusion.15
  437.8 2.1 fusion.185
  439.9 1.3 fusion.186
  441.2 1.3 copy.108
  443.2 1.1 constant_dynamic-update-slice_fusion.3
  449.2 2.1 fusion.185
  451.4 1.3 fusion.186
  452.7 1.3 copy.108
  460.7 2.1 fusion.185
  462.8 1.3 fusion.186
  464.1 1.3 copy.108
  468.3 30.6 %all-gather.17.cloned.1.call-done = bf16[128,4,2048]{2,1,0:T(4,128)(2,1)} async-done(((bf16[1,4,2048]{2,1,0:T(4,128)(2,1)}), bf16[128,4,2048]{2,1,0:T(4,128)(2,1)}) %all-gather.17.cloned.1.call-update) | async-done | bytes 2097168 | tf_op jit(solution)/shard_map/all_gather | solution.py:78
  498.9 2.5 reshape.481
  501.5 4.0 multiply_convert_fusion
  505.5 187.8 %all-gather.13.cloned.1.call-done = bf16[2048,512]{1,0:T(8,128)(2,1)} async-done(((bf16[16,512]{1,0:T(8,128)(2,1)}), bf16[2048,512]{1,0:T(8,128)(2,1)}) %all-gather.13.cloned.1.call-update) | async-done | bytes 2097168 | tf_op jit(solution)/shard_map/all_gather | solution.py:80
  693.3 3.7 convert_reduce_fusion
  697.0 2.8 fusion.96
  700.5 1.3 fusion.73
  701.7 63.1 %reduce-scatter.4.cloned.1.call-done = bf16[128,512]{1,0:T(8,128)(2,1)} async-done(((bf16[2048,512]{1,0:T(8,128)(2,1)}), bf16[128,512]{1,0:T(8,128)(2,1)}) %reduce-scatter.4.cloned.1.call-update) | async-done | bytes 131088 | tf_op jit(solution)/shard_map/reduce_scatter | solution.py:225
  767.6 71.6 %reduce-scatter.6.cloned.1.call-done = bf16[128,512]{1,0:T(8,128)(2,1)} async-done(((bf16[2048,512]{1,0:T(8,128)(2,1)}), bf16[128,512]{1,0:T(8,128)(2,1)}) %reduce-scatter.6.cloned.1.call-update) | async-done | bytes 131088 | tf_op jit(solution)/shard_map/reduce_scatter | solution.py:228
  841.8 3.0 fusion.68
  844.9 2.7 fusion.71
  848.2 2.0 fusion.106
  850.6 2.3 fusion.34
  855.2 67.3 %all-reduce.26 = (f32[512]{0:T(512)S(1)}, f32[512]{0:T(512)S(1)}, f32[512]{0:T(512)S(1)}, f32[512]{0:T(512)S(1)}, f32[1024]{0:T(1024)S(1)}, /*index=5*/f32[512]{0:T(512)S(1)}, f32[512]{0:T(512)S(1)}, f32[2048]{0:T(1024)S(1)}) all-reduce(f32[512]{0:T(512)S(1)} %get-tuple-element.546, ...), channel_id=4, replica_groups=mesh['dp'=8,'ctx'=16] {'dp','ctx'}, use_global_device_ids=true, to_apply=%region_21.22.clone | all-reduce | flops 6144 | bytes 49152
  927.1 81.3 %all-reduce.31.cloned.1.call-done = (f32[512,1536]{1,0:T(8,128)}, f32[512,512]{1,0:T(8,128)}, f32[512,2048]{1,0:T(8,128)}) async-done(((f32[512,1536]{1,0:T(8,128)}, f32[512,512]{1,0:T(8,128)}, f32[512,2048]{1,0:T(8,128)}), (f32[512,1536]{1,0:T(8,128)}, f32[512,512]{1,0:T(8,128)}, f32[512,2048]{1,0:T(8,128)})) %all-reduce.31.cloned.1.call-update) | async-done | bytes 8388624
  1008.4 1.3 constant_dynamic-slice_fusion.6
  1009.7 1.4 constant_dynamic-slice_fusion.7
  1011.1 1.5 constant_dynamic-slice_fusion.5
  1012.6 635.0 %reduce-scatter.8.cloned.1.call-done = f32[16,512]{1,0:T(8,128)} async-done(((f32[2048,512]{1,0:T(8,128)}), f32[16,512]{1,0:T(8,128)}) %reduce-scatter.8.cloned.1.call-update) | async-done | bytes 32784 | tf_op jit(solution)/shard_map/reduce_scatter | solution.py:259
  (328 shorter events, 66.5 us)
Async XLA Ops:
  7.2 201.8 %copy-start.3 = (bf16[1,128,512]{2,1,0:T(8,128)(2,1)S(1)}, bf16[1,128,512]{2,1,0:T(8,128)(2,1)}, u32[]{:S(2)}) copy-start(bf16[1,128,512]{2,1,0:T(8,128)(2,1)} %param.21) | copy-start | bytes 393220
  7.2 199.0 %all-gather.15.cloned.1.call-start = ((), (), s32[]{:S(2)}) async-start(), calls=%async_computation.9 | async-start | bytes 1585152 | tf_op jit(solution)/shard_map/all_gather | solution.py:74
  7.9 383.4 %all-gather.11.cloned.1.call-start = ((), (), s32[]{:S(2)}) async-start(), calls=%async_computation.4 | async-start | bytes 2228224 | tf_op jit(solution)/shard_map/all_gather | solution.py:120
  83.0 126.4 %copy-start.24 = (f32[512]{0:T(512)}, f32[512]{0:T(512)S(1)}, u32[]{:S(2)}) copy-start(f32[512]{0:T(512)S(1)} %convert_element_type.139) | copy-start | bytes 6148
  83.8 126.4 %copy-start.17 = (f32[128,16]{0,1:T(8,128)}, f32[128,16]{0,1:T(8,128)S(1)}, u32[]{:S(2)}) copy-start(f32[128,16]{0,1:T(8,128)S(1)} %get-tuple-element.657) | copy-start | bytes 24580
  83.8 126.4 %copy-start.19 = (f32[128,16]{0,1:T(8,128)}, f32[128,16]{0,1:T(8,128)S(1)}, u32[]{:S(2)}) copy-start(f32[128,16]{0,1:T(8,128)S(1)} %get-tuple-element.658) | copy-start | bytes 24580
  84.9 124.6 %copy-start.21 = (f32[128]{0:T(128)}, f32[128]{0:T(128)S(1)}, u32[]{:S(2)}) copy-start(f32[128]{0:T(128)S(1)} %broadcast_multiply_fusion.1) | copy-start | bytes 1540
  86.0 123.5 %copy-start.33 = (f32[128]{0:T(128)}, f32[128]{0:T(128)S(1)}, u32[]{:S(2)}) copy-start(f32[128]{0:T(128)S(1)} %fusion.59) | copy-start | bytes 1540
  86.0 123.5 %copy-start.25 = (f32[128]{0:T(128)}, f32[128]{0:T(128)S(1)}, u32[]{:S(2)}) copy-start(f32[128]{0:T(128)S(1)} %fusion.95) | copy-start | bytes 1540
  209.5 3.5 copy-start.16
  209.5 3.6 copy-start.29
  209.8 181.1 %copy-start.10 = (bf16[1,128,512]{2,1,0:T(8,128)(2,1)S(1)}, bf16[1,128,512]{2,1,0:T(8,128)(2,1)}, u32[]{:S(2)}) copy-start(bf16[1,128,512]{2,1,0:T(8,128)(2,1)} %param.35) | copy-start | bytes 393220
  211.0 195.2 %all-gather.9.cloned.1.call-start = ((), (), s32[]{:S(2)}) async-start(), calls=%async_computation.3 | async-start | bytes 2228224 | tf_op jit(solution)/shard_map/all_gather | solution.py:121
  211.7 287.2 %all-gather.17.cloned.1.call-start = ((), (), s32[]{:S(2)}) async-start(), calls=%async_computation.10 | async-start | bytes 2113536 | tf_op jit(solution)/shard_map/all_gather | solution.py:78
  212.3 481.0 %all-gather.13.cloned.1.call-start = ((), (), s32[]{:S(2)}) async-start(), calls=%async_computation.5 | async-start | bytes 2113536 | tf_op jit(solution)/shard_map/all_gather | solution.py:80
  212.9 551.9 %reduce-scatter.4.cloned.1.call-start = ((), (), s32[]{:S(2)}) async-start(), calls=%async_computation.6 | async-start | bytes 2228224 | tf_op jit(solution)/shard_map/reduce_scatter | solution.py:225
  421.5 3.3 copy-start.31
  421.5 3.3 copy-start.38
  423.8 2.1 copy-start
  432.8 3.3 copy-start.31
  432.8 3.3 copy-start.38
  435.2 2.1 copy-start
  443.0 1.3 copy-start.32
  444.3 3.3 copy-start.31
  444.3 3.3 copy-start.38
  446.6 2.1 copy-start
  455.7 3.3 copy-start.31
  455.7 3.3 copy-start.38
  458.1 2.1 copy-start
  467.2 372.0 %reduce-scatter.6.cloned.1.call-start = ((), (), s32[]{:S(2)}) async-start(), calls=%async_computation.7 | async-start | bytes 2228224 | tf_op jit(solution)/shard_map/reduce_scatter | solution.py:228
  468.0 540.4 %all-reduce.31.cloned.1.call-start = ((), (), s32[]{:S(2)}) async-start(), calls=%async_computation.11 | async-start | bytes 16777216
  468.3 33.2 %copy-start.22 = (f32[128]{0:T(128)S(1)}, f32[128]{0:T(128)}, u32[]{:S(2)}) copy-start(f32[128]{0:T(128)} %copy-done.21) | copy-start | bytes 1540
  468.3 33.2 %copy-start.26 = (f32[128]{0:T(128)S(1)}, f32[128]{0:T(128)}, u32[]{:S(2)}) copy-start(f32[128]{0:T(128)} %copy-done.25) | copy-start | bytes 1540
  501.5 191.8 %copy-start.11 = (bf16[1,128,512]{2,1,0:T(8,128)(2,1)S(1)}, bf16[1,128,512]{2,1,0:T(8,128)(2,1)}, u32[]{:S(2)}) copy-start(bf16[1,128,512]{2,1,0:T(8,128)(2,1)} %param.35) | copy-start | bytes 393220
  505.5 339.4 %copy-start.9 = (bf16[128,2048]{1,0:T(8,128)(2,1)}, bf16[128,2048]{1,0:T(8,128)(2,1)S(1)}, u32[]{:S(2)}) copy-start(bf16[128,2048]{1,0:T(8,128)(2,1)S(1)} %get-tuple-element.629) | copy-start | bytes 1572868
  697.0 2.8 copy-start.13
  697.0 2.8 copy-start.15
  697.0 2.8 copy-start.4
  699.7 66.8 %copy-start.18 = (f32[128,16]{0,1:T(8,128)S(1)}, f32[128,16]{0,1:T(8,128)}, u32[]{:S(2)}) copy-start(f32[128,16]{0,1:T(8,128)} %copy-done.17) | copy-start | bytes 24580
  844.9 802.7 %reduce-scatter.8.cloned.1.call-start = ((), (), s32[]{:S(2)}) async-start(), calls=%async_computation.8 | async-start | bytes 4227072 | tf_op jit(solution)/shard_map/reduce_scatter | solution.py:259
  847.6 2.6 copy-start.6
  848.2 2.3 copy-start.12
  850.3 2.7 copy-start.20
  850.3 2.8 copy-start.2
  850.3 2.8 copy-start.8
  850.3 2.8 copy-start.23
  850.6 3.3 copy-start.34
  853.1 2.1 copy-start.28
  (16 other events, 17.3 us)
Sparse Core Ops, SparseCore 0:
  9.7 196.4 all-gather.14
  211.1 46.2 all-gather.10
  260.3 45.1 all-gather.8
  307.0 191.8 all-gather.16
  500.5 192.7 all-gather.12
  697.0 67.7 reduce-scatter.3
  769.2 69.9 reduce-scatter.5
  845.0 163.3 all-reduce.30
  1011.5 636.0 reduce-scatter.7
where the time goes:
time: 1660 us; the launch traced here: 1650 us
  waiting for transfers between devices  1190 us (72%)
  blocking collectives  313 us (19%)
  local copies, waits for them, and re-layouts  62.9 us (4%)
  matrix products  49.5 us (3%)
    reduce_scatter x1, waiting for transfers between devices, per_device(): lax.psum_scatter(grad_w_down, ('dp', 'ctx'), scatter_dimension=0, tiled=T...  635 us
    all_gather x1, waiting for transfers between devices, per_device(): lax.all_gather(down_weight, ('dp', 'ctx'), axis=0, tiled=True)  188 us
    all_gather x1, blocking collectives, per_device(): lax.all_gather(attn_out_weight, ('dp', 'ctx'), axis=0, tiled=True)  177 us
    unnamed x2, blocking collectives  136 us
    all_gather x1, waiting for transfers between devices, per_device(): lax.all_gather(qkv_weight, ('dp', 'ctx'), axis=0, tiled=True)  120 us
    unnamed x10, waiting for transfers between devices  83.8 us
    reduce_scatter x1, waiting for transfers between devices, per_device(): lax.psum_scatter(d_val_all.astype(jnp.bfloat16), 'ctx', scatter_dimension...  71.6 us
    reduce_scatter x1, waiting for transfers between devices, per_device(): lax.psum_scatter(d_key_all.astype(jnp.bfloat16), 'ctx', scatter_dimension...  63.1 us
  transfers between devices with their start and end apart: 9, of which 7 were waited for; matrix products, arithmetic and copies ran while one was open for 7% of the time, Pallas kernels for 0%

commit v1 on v0

v1 whole, which is shorter than its diff:
```python
import jax
import jax.numpy as jnp
from jax import lax
from jax.experimental import pallas as pl
from jax.experimental.pallas import tpu as pltpu
from jax.sharding import PartitionSpec as P

HEAD_DIM = 64
ROT_DIM = 16
EPS = 1e-05
MESH = pl.DeviceIdType.MESH
F32 = jnp.float32
BF16 = jnp.bfloat16
VMEM = pltpu.VMEM
LIMIT = 56 * 1024 * 1024

STREAMS = 7
TILES = [((16, 256), BF16)] * 6 + [((8, 128), F32)]


def coords(dp, ctx):
    z = lax.div(dp, 2)
    x = lax.rem(lax.div(ctx, 2), 2) * 2 + lax.rem(dp, 2)
    y = lax.div(ctx, 4)
    return z, x, y, lax.rem(ctx, 2)


def device_of(z, x, y, core):
    return (z * 2 + lax.rem(x, 2), y * 4 + lax.div(x, 2) * 2 + core)


def gray_bits(z, x, y):
    out = []
    for i in (x, y, z):
        hi = lax.div(i, 2)
        out += [lax.rem(hi + i, 2), hi]
    return out


def slot_of(p, bits):
    return sum(bits[(p + k) % 6] * 2**k for k in range(6))


def partner(j, z, x, y):
    def turn(i):
        return 3 - i if j % 2 else i + 1 - 2 * lax.rem(i, 2)

    if j < 2:
        return z, turn(x), y
    if j < 4:
        return z, x, turn(y)
    return turn(z), x, y


def quad_peer(delta, x, core):
    core_t = 1 - core if delta % 2 else core
    x_t = lax.rem(x + 2, 4) if delta // 2 else x
    return x_t, core_t, lax.div(x_t, 2) * 2 + core_t


def enter(peers):
    barrier = pltpu.get_barrier_semaphore()
    for peer in peers:
        pl.semaphore_signal(barrier, inc=1, device_id=peer, device_id_type=MESH)
    pl.semaphore_wait(barrier, len(peers))


def send(src, dst, ssem, rsem, peer):
    copy = pltpu.make_async_remote_copy(
        src_ref=src, dst_ref=dst, send_sem=ssem, recv_sem=rsem, device_id=peer, device_id_type=MESH
    )
    copy.start()
    return copy


def weight_peers(z, x, y, core):
    peers = [device_of(*partner(j, z, x, y), core) for j in range(6)]
    for delta in (1, 2, 3):
        x_t, core_t, _ = quad_peer(delta, x, core)
        peers.append(device_of(z, x_t, y, core_t))
    return peers


def gather_kernel(wa_ref, wd_ref, sm_ref, wa_out, wd_out, sm_out, *rest):
    bufs = rest[:STREAMS]
    squad, rquad, asm, qs, qr, ss, rs, fs, fr = rest[STREAMS:]
    z, x, y, core = coords(lax.axis_index("dp"), lax.axis_index("ctx"))
    bits = gray_bits(z, x, y)
    q = lax.div(x, 2) * 2 + core
    squad[...] = jnp.zeros_like(squad)
    own = wa_ref[...].astype(F32)
    for t in range(4):
        squad[t, 0:4, :] = own[:, 1024 * t : 1024 * (t + 1)]
    enter(weight_peers(z, x, y, core))
    quad = []
    for delta in (1, 2, 3):
        x_t, core_t, q_t = quad_peer(delta, x, core)
        quad.append(
            send(
                squad.at[q_t], rquad.at[q], qs.at[delta - 1], qr.at[delta - 1],
                device_of(z, x_t, y, core_t),
            )
        )
    rquad[q] = squad[q]
    slots = [slot_of(p, bits) for p in range(STREAMS)]
    bufs[4][core, slots[4]] = wd_ref[:, 0:256]
    bufs[5][core, slots[5]] = wd_ref[:, 256:512]
    bufs[6][core, slots[6]] = sm_ref[...]
    for copy in quad:
        copy.wait_recv()
    for t in range(4):
        asm[4 * t : 4 * t + 4, :] = rquad[t, 0:4, :]
    for p in range(4):
        bufs[p][core, slots[p]] = asm[:, 256 * p : 256 * (p + 1)].astype(BF16)
    sibling = device_of(z, x, y, 1 - core)
    steps, forwards = {}, {}
    for k in range(7):
        for p in (4, 5, 6, 0, 1, 2, 3):
            if k > 0:
                steps[p, k - 1].wait_recv()
            if k < 6:
                size = 2**k
                base = lax.div(slots[p], size) * size
                part = bufs[p].at[core, pl.ds(base, size)]
                peer = device_of(*partner((p + k) % 6, z, x, y), core)
                steps[p, k] = send(part, part, ss.at[p, k], rs.at[p, k], peer)
            if k == 0:
                fresh = bufs[p].at[core, pl.ds(slots[p], 1)]
            else:
                size = 2 ** (k - 1)
                base = lax.div(slots[p], size) * size
                base = base + size * (1 - 2 * bits[(p + k - 1) % 6])
                fresh = bufs[p].at[core, pl.ds(base, size)]
            forwards[p, k] = send(fresh, fresh, fs.at[p, k], fr.at[p, k], sibling)
    for copy in forwards.values():
        copy.wait_recv()
    for copy in quad + list(steps.values()) + list(forwards.values()):
        copy.wait_send()

    def unpack(row, carry):
        for t in range(4):
            z_i = lax.div(row, 8)
            x_i = (t // 2) * 2 + lax.rem(lax.div(row, 4), 2)
            b_i = gray_bits(z_i, x_i, lax.rem(row, 4))
            at = [slot_of(p, b_i) for p in range(STREAMS)]
            rows = pl.ds(pl.multiple_of(row * 16, 16), 16)
            for p in range(4):
                left = 1024 * t + 256 * p
                wa_out[rows, left : left + 256] = bufs[p][t % 2, at[p]]
            rows = pl.ds(pl.multiple_of(row * 64 + t * 16, 16), 16)
            wd_out[rows, 0:256] = bufs[4][t % 2, at[4]]
            wd_out[rows, 256:512] = bufs[5][t % 2, at[5]]
            sm_out[row * 4 + t] = bufs[6][t % 2, at[6]]
        return carry

    lax.fori_loop(0, 32, unpack, 0)


def gather_weights(wa, wd, sm):
    scratch = [VMEM((2, 64) + tile, dtype) for tile, dtype in TILES]
    scratch += [VMEM((4, 8, 1024), F32), VMEM((4, 8, 1024), F32), VMEM((16, 1024), F32)]
    dma = pltpu.SemaphoreType.DMA
    scratch += [dma((3,)), dma((3,)), dma((7, 6)), dma((7, 6)), dma((7, 7)), dma((7, 7))]
    return pl.pallas_call(
        gather_kernel,
        out_shape=(
            jax.ShapeDtypeStruct((512, 4096), BF16),
            jax.ShapeDtypeStruct((2048, 512), BF16),
            jax.ShapeDtypeStruct((128, 8, 128), F32),
        ),
        in_specs=[pl.BlockSpec(memory_space=VMEM)] * 3,
        out_specs=[pl.BlockSpec(memory_space=VMEM)] * 3,
        scratch_shapes=scratch,
        compiler_params=pltpu.CompilerParams(
            collective_id=0, has_side_effects=True, vmem_limit_bytes=LIMIT
        ),
    )(wa, wd, sm)


def reduce_kernel(wa_ref, wd_ref, sm_ref, qkv_out, proj_out, up_out, wd_out, sm_out, *rest):
    bufs = rest[:STREAMS]
    recv = rest[STREAMS : 2 * STREAMS]
    squad, rquad, asm, qs, qr, ss, rs, fs, fr = rest[2 * STREAMS :]
    z, x, y, core = coords(lax.axis_index("dp"), lax.axis_index("ctx"))
    bits = gray_bits(z, x, y)
    q = lax.div(x, 2) * 2 + core
    slots = [slot_of(p, bits) for p in range(STREAMS)]

    def pack(row, carry):
        for t in range(4):
            z_i = lax.div(row, 8)
            x_i = (t // 2) * 2 + lax.rem(lax.div(row, 4), 2)
            b_i = gray_bits(z_i, x_i, lax.rem(row, 4))
            at = [slot_of(p, b_i) for p in range(STREAMS)]
            rows = pl.ds(pl.multiple_of(row * 16, 16), 16)
            for p in range(4):
                left = 1024 * t + 256 * p
                bufs[p][t % 2, at[p]] = wa_ref[rows, left : left + 256]
            rows = pl.ds(pl.multiple_of(row * 64 + t * 16, 16), 16)
            bufs[4][t % 2, at[4]] = wd_ref[rows, 0:256]
            bufs[5][t % 2, at[5]] = wd_ref[rows, 256:512]
            bufs[6][t % 2, at[6]] = sm_ref[row * 4 + t]
        return carry

    lax.fori_loop(0, 32, pack, 0)
    enter(weight_peers(z, x, y, core))
    sibling = device_of(z, x, y, 1 - core)
    forwards = [
        send(bufs[p].at[1 - core], recv[p].at[pl.ds(0, 64)], fs.at[p], fr.at[p], sibling)
        for p in range(STREAMS)
    ]
    steps = {}

    def add(p, base, off, count):
        unit = min(count, 4)

        def body(i, carry):
            here = pl.ds(base + i * unit, unit)
            there = pl.ds(off + i * unit, unit)
            bufs[p][core, here] = bufs[p][core, here] + recv[p][there]
            return carry

        lax.fori_loop(0, count // unit, body, 0)

    for k in range(6, -1, -1):
        size = 2**k
        for p in range(STREAMS):
            if k == 6:
                forwards[p].wait_recv()
                add(p, 0, 0, 64)
            else:
                steps[p, k].wait_recv()
                if k > 0:
                    base = lax.div(slots[p], size) * size
                    add(p, base, 128 - 2 * size, size)
            if k > 0:
                half = size // 2
                base = lax.div(slots[p], half) * half
                base = base + half * (1 - 2 * bits[(p + k - 1) % 6])
                peer = device_of(*partner((p + k - 1) % 6, z, x, y), core)
                steps[p, k - 1] = send(
                    bufs[p].at[core, pl.ds(base, half)],
                    recv[p].at[pl.ds(128 - 2 * half, half)],
                    ss.at[p, k - 1], rs.at[p, k - 1], peer,
                )
    last = [
        bufs[p][core, slots[p]].astype(F32) + recv[p][126].astype(F32) for p in range(STREAMS)
    ]
    for p in range(4):
        asm[:, 256 * p : 256 * (p + 1)] = last[p]
    wd_out[:, 0:256] = last[4]
    wd_out[:, 256:512] = last[5]
    sm_out[...] = last[6]
    squad[...] = jnp.zeros_like(squad)
    for t in range(4):
        squad[t, 0:4, :] = asm[4 * t : 4 * t + 4, :]
    quad = []
    for delta in (1, 2, 3):
        x_t, core_t, q_t = quad_peer(delta, x, core)
        quad.append(
            send(
                squad.at[q_t], rquad.at[q], qs.at[delta - 1], qr.at[delta - 1],
                device_of(z, x_t, y, core_t),
            )
        )
    rquad[q] = squad[q]
    for copy in quad:
        copy.wait_recv()
    qkv_out[:, 0:1024] = rquad[0, 0:4, :]
    qkv_out[:, 1024:1536] = rquad[1, 0:4, 0:512]
    proj_out[...] = rquad[1, 0:4, 512:1024]
    up_out[:, 0:1024] = rquad[2, 0:4, :]
    up_out[:, 1024:2048] = rquad[3, 0:4, :]
    for copy in quad + list(steps.values()) + forwards:
        copy.wait_send()


def reduce_grads(wa, wd, sm):
    scratch = [VMEM((2, 64) + tile, dtype) for tile, dtype in TILES]
    scratch += [VMEM((128,) + tile, dtype) for tile, dtype in TILES]
    scratch += [VMEM((4, 8, 1024), F32), VMEM((4, 8, 1024), F32), VMEM((16, 1024), F32)]
    dma = pltpu.SemaphoreType.DMA
    scratch += [dma((3,)), dma((3,)), dma((7, 6)), dma((7, 6)), dma((7,)), dma((7,))]
    return pl.pallas_call(
        reduce_kernel,
        out_shape=(
            jax.ShapeDtypeStruct((4, 1536), F32),
            jax.ShapeDtypeStruct((4, 512), F32),
            jax.ShapeDtypeStruct((4, 2048), F32),
            jax.ShapeDtypeStruct((16, 512), F32),
            jax.ShapeDtypeStruct((8, 128), F32),
        ),
        in_specs=[pl.BlockSpec(memory_space=VMEM)] * 3,
        out_specs=[pl.BlockSpec(memory_space=VMEM)] * 5,
        scratch_shapes=scratch,
        compiler_params=pltpu.CompilerParams(
            collective_id=1, has_side_effects=True, vmem_limit_bytes=LIMIT
        ),
    )(wa, wd, sm)


def head_peer(delta, ctx):
    y, x_hi, core = lax.div(ctx, 4), lax.rem(lax.div(ctx, 2), 2), lax.rem(ctx, 2)
    if delta % 2:
        x_hi = 1 - x_hi
    if delta // 2 == 1:
        y = y + 1 - 2 * lax.rem(y, 2)
    elif delta // 2 == 2:
        y = lax.rem(y + 2, 4)
    elif delta // 2 == 3:
        y = 3 - y
    return y * 2 + x_hi, core


def head_peers(dp, ctx):
    peers = []
    for delta in range(1, 8):
        m, core = head_peer(delta, ctx)
        peers.append((dp, m * 2 + core))
    m, core = head_peer(0, ctx)
    return peers + [(dp, m * 2 + 1 - core)]


def spread_kernel(x_ref, y_ref, ss, rs, fs, fr):
    dp, ctx = lax.axis_index("dp"), lax.axis_index("ctx")
    core, me = lax.rem(ctx, 2), lax.div(ctx, 2)
    peers = head_peers(dp, ctx)
    enter(peers)
    sends = []
    for delta in range(1, 8):
        m, _ = head_peer(delta, ctx)
        sends.append(
            send(
                x_ref.at[m], y_ref.at[core, me], ss.at[delta - 1], rs.at[delta - 1],
                peers[delta - 1],
            )
        )
    y_ref[core, me] = x_ref[me]
    mine = y_ref.at[core, me]
    forwards = [send(mine, mine, fs.at[0], fr.at[0], peers[7])]
    for delta in range(1, 8):
        m, _ = head_peer(delta, ctx)
        sends[delta - 1].wait_recv()
        part = y_ref.at[core, m]
        forwards.append(send(part, part, fs.at[delta], fr.at[delta], peers[7]))
    for copy in forwards:
        copy.wait_recv()
    for copy in sends + forwards:
        copy.wait_send()


def spread_heads(x):
    dma = pltpu.SemaphoreType.DMA
    return pl.pallas_call(
        spread_kernel,
        out_shape=jax.ShapeDtypeStruct((2, 8, 128, 256), BF16),
        in_specs=[pl.BlockSpec(memory_space=VMEM)],
        out_specs=pl.BlockSpec(memory_space=VMEM),
        scratch_shapes=[dma((7,)), dma((7,)), dma((8,)), dma((8,))],
        compiler_params=pltpu.CompilerParams(
            collective_id=2, has_side_effects=True, vmem_limit_bytes=LIMIT
        ),
    )(x)


def collect_kernel(z_ref, o_ref, recv, total, ss, rs, fs, fr):
    dp, ctx = lax.axis_index("dp"), lax.axis_index("ctx")
    core, me = lax.rem(ctx, 2), lax.div(ctx, 2)
    peers = head_peers(dp, ctx)
    enter(peers)
    forwards = []
    for delta in (1, 2, 3, 4, 5, 6, 7, 0):
        m, _ = head_peer(delta, ctx)
        forwards.append(
            send(z_ref.at[1 - core, m], recv.at[m], fs.at[delta], fr.at[delta], peers[7])
        )
    sends = []
    for delta in (1, 2, 3, 4, 5, 6, 7, 0):
        m, _ = head_peer(delta, ctx)
        forwards[delta - 1].wait_recv()
        total[m] = z_ref[core, m] + recv[m]
        if delta:
            sends.append(
                send(
                    total.at[m], o_ref.at[me], ss.at[delta - 1], rs.at[delta - 1],
                    peers[delta - 1],
                )
            )
        else:
            o_ref[me] = total[m]
    for copy in sends:
        copy.wait_recv()
    for copy in sends + forwards:
        copy.wait_send()


def collect_heads(z):
    dma = pltpu.SemaphoreType.DMA
    return pl.pallas_call(
        collect_kernel,
        out_shape=jax.ShapeDtypeStruct((8, 128, 256), BF16),
        in_specs=[pl.BlockSpec(memory_space=VMEM)],
        out_specs=pl.BlockSpec(memory_space=VMEM),
        scratch_shapes=[
            VMEM((8, 128, 256), BF16), VMEM((8, 128, 256), BF16),
            dma((7,)), dma((7,)), dma((8,)), dma((8,)),
        ],
        compiler_params=pltpu.CompilerParams(
            collective_id=3, has_side_effects=True, vmem_limit_bytes=LIMIT
        ),
    )(z)


def nt(a, b):
    return lax.dot_general(a, b, (((1,), (1,)), ((), ())), preferred_element_type=F32)


def nn(a, b):
    return lax.dot_general(a, b, (((1,), (0,)), ((), ())), preferred_element_type=F32)


def tn(a, b):
    return lax.dot_general(a, b, (((0,), (0,)), ((), ())), preferred_element_type=F32)


def attend_kernel(order_ref, y_ref, z_ref, qb, kb, vb, db, att_b, dq_b, dk_b, dv_b):
    core = lax.rem(lax.axis_index("ctx"), 2)
    for s in range(32):
        there = pl.ds(pl.multiple_of(order_ref[s] * 64, 64), 64)
        part = y_ref[(s // 2) % 2, s // 4, 64 * (s % 2) : 64 * (s % 2) + 64, :]
        qb[there, :] = part[:, 0:64]
        kb[there, :] = part[:, 64:128]
        vb[there, :] = part[:, 128:192]
        db[there, :] = part[:, 192:256]
    att_b[...] = jnp.zeros_like(att_b)
    dq_b[...] = jnp.zeros_like(dq_b)
    dk_b[...] = jnp.zeros_like(dk_b)
    dv_b[...] = jnp.zeros_like(dv_b)
    for j in range(4):
        width = 512 * (j + 1)
        row = 512 * j + 256 * (1 - core if j % 2 else core)
        rows = pl.ds(pl.multiple_of(row, 256), 256)
        queries = qb[rows, :] * jnp.asarray(0.125, BF16)
        d_o = db[rows, :]
        keys, vals = kb[0:width, :], vb[0:width, :]
        scores = nt(queries, keys)
        at_q = row + lax.broadcasted_iota(jnp.int32, (256, width), 0)
        at_k = lax.broadcasted_iota(jnp.int32, (256, width), 1)
        scores = jnp.where(at_q >= at_k, scores, -1e30)
        probs = jnp.exp(scores - jnp.max(scores, axis=1, keepdims=True))
        probs = probs * (1.0 / jnp.sum(probs, axis=1, keepdims=True))
        low = probs.astype(BF16)
        att = nn(low, vals)
        delta = jnp.sum(d_o.astype(F32) * att, axis=1, keepdims=True)
        d_s = (probs * (nt(d_o, vals) - delta)).astype(BF16)
        att_b[rows, :] = att
        dq_b[rows, :] = nn(d_s, keys) * 0.125
        dk_b[0:width, :] += tn(d_s, queries)
        dv_b[0:width, :] += tn(low, d_o)
    for s in range(32):
        here = pl.ds(pl.multiple_of(order_ref[s] * 64, 64), 64)
        z_ref[(s // 2) % 2, s // 4, 64 * (s % 2) : 64 * (s % 2) + 64, :] = jnp.concatenate(
            [att_b[here, :], dq_b[here, :], dk_b[here, :], dv_b[here, :]], axis=1
        ).astype(BF16)


def attend(order, y):
    return pl.pallas_call(
        attend_kernel,
        out_shape=jax.ShapeDtypeStruct((2, 8, 128, 256), BF16),
        in_specs=[pl.BlockSpec(memory_space=pltpu.SMEM), pl.BlockSpec(memory_space=VMEM)],
        out_specs=pl.BlockSpec(memory_space=VMEM),
        scratch_shapes=[VMEM((2048, 64), BF16)] * 4 + [VMEM((2048, 64), F32)] * 4,
        compiler_params=pltpu.CompilerParams(vmem_limit_bytes=LIMIT),
    )(order, y)


def layer_norm(values, gain, shift):
    center = values - jnp.mean(values, axis=-1, keepdims=True)
    spread = jnp.mean(center * center, axis=-1, keepdims=True)
    return center * lax.rsqrt(spread + EPS) * gain + shift


def rotary(tensor, places):
    half_rot = ROT_DIM // 2
    freqs = 10000.0 ** (-jnp.arange(half_rot, dtype=jnp.float32) * 2.0 / ROT_DIM)
    angle = places.astype(jnp.float32)[:, None] * freqs[None, :]
    angle = jnp.concatenate([angle, angle], axis=-1)[:, None, :]
    turned_part = tensor[..., :ROT_DIM]
    swapped = jnp.concatenate([-turned_part[..., half_rot:], turned_part[..., :half_rot]], axis=-1)
    return jnp.concatenate(
        [turned_part * jnp.cos(angle) + swapped * jnp.sin(angle), tensor[..., ROT_DIM:]], axis=-1
    )


def per_device(
    hidden_in, positions, block_order, norm1_gain, norm1_bias, norm2_gain, norm2_bias,
    qkv_weight, qkv_bias, attn_out_weight, out_bias, up_weight, up_bias, down_weight, out_grad,
):
    small = jnp.concatenate(
        [norm1_gain, norm1_bias, norm2_gain, norm2_bias, qkv_bias, out_bias, up_bias]
    ).astype(F32)
    small = jnp.pad(small[None], ((0, 7), (0, 80)))
    wide = jnp.concatenate([qkv_weight, attn_out_weight, up_weight], axis=1)
    w_all, w_down, smalls = gather_weights(wide, down_weight, small)
    w_qkv, w_out, w_up = w_all[:, :1536], w_all[:, 1536:2048], w_all[:, 2048:]
    smalls = smalls[:, 0, :48]
    gain_one, shift_one, gain_two, shift_two = (
        smalls[:, 4 * i : 4 * i + 4].reshape(512) for i in range(4)
    )
    b_qkv = smalls[:, 16:28].reshape(1536)
    b_out = smalls[:, 28:32].reshape(512)
    b_up = smalls[:, 32:48].reshape(2048)

    inputs = hidden_in[0].astype(F32)
    grad_out = out_grad[0]
    nrows, width = inputs.shape
    places = positions[0]

    def norms(values, g_one, s_one, g_two, s_two):
        return (layer_norm(values, g_one, s_one), layer_norm(values, g_two, s_two))

    (normed_one, normed_two), norm_pull = jax.vjp(
        norms, inputs, gain_one, shift_one, gain_two, shift_two
    )
    normed_one = normed_one.astype(BF16)
    normed_two = normed_two.astype(BF16)
    qkv = (nn(normed_one, w_qkv) + b_qkv).reshape(nrows, 3, 8, 64)

    def turn_both(q_part, k_part):
        return (rotary(q_part, places), rotary(k_part, places))

    (q_turned, k_turned), turn_pull = jax.vjp(turn_both, qkv[:, 0], qkv[:, 1])
    d_mixed = nt(grad_out, w_out).astype(BF16).reshape(nrows, 8, 64)
    heads = jnp.stack(
        [q_turned.astype(BF16), k_turned.astype(BF16), qkv[:, 2].astype(BF16), d_mixed], axis=2
    )
    heads = heads.transpose(1, 0, 2, 3).reshape(8, nrows, 256)
    back = collect_heads(attend(block_order, spread_heads(heads)))
    back = back.reshape(8, nrows, 4, 64).transpose(2, 1, 0, 3)
    mixed_att = back[0].reshape(nrows, width)

    upper = nn(normed_two, w_up) + b_up
    gelu_val, gelu_pull = jax.vjp(lambda arg_in: jax.nn.gelu(arg_in, approximate=False), upper)
    gelu_out = gelu_val.astype(BF16)
    result = inputs + nn(mixed_att, w_out) + nn(gelu_out, w_down) + b_out
    block_out = result.astype(BF16)[None]
    grad_w_out = tn(mixed_att, grad_out)
    grad_w_down = tn(gelu_out, grad_out)
    grad_b_out = jnp.sum(grad_out.astype(F32), axis=0)
    d_upper = gelu_pull(nt(grad_out, w_down))[0].astype(BF16)
    grad_w_up = tn(normed_two, d_upper)
    grad_b_up = jnp.sum(d_upper.astype(F32), axis=0)
    d_normed_two = nt(d_upper, w_up)
    d_q_pre, d_k_pre = turn_pull((back[1].astype(F32), back[2].astype(F32)))
    d_qkv = (
        jnp.stack([d_q_pre, d_k_pre, back[3].astype(F32)], axis=1)
        .reshape(nrows, 3 * width)
        .astype(BF16)
    )
    grad_w_qkv = tn(normed_one, d_qkv)
    grad_b_qkv = jnp.sum(d_qkv.astype(F32), axis=0)
    d_normed_one = nt(d_qkv, w_qkv)
    d_inputs, grad_g_one, grad_s_one, grad_g_two, grad_s_two = norm_pull(
        (d_normed_one, d_normed_two)
    )
    input_grad = (grad_out.astype(F32) + d_inputs)[None]
    wide_grad = jnp.concatenate([grad_w_qkv, grad_w_out, grad_w_up], axis=1).astype(BF16)
    small_grad = jnp.concatenate(
        [
            item.reshape(128, -1)
            for item in (
                grad_g_one, grad_s_one, grad_g_two, grad_s_two,
                grad_b_qkv[:1024], grad_b_qkv[1024:], grad_b_out, grad_b_up,
            )
        ],
        axis=1,
    )
    small_grad = jnp.pad(small_grad[:, None, :], ((0, 0), (0, 7), (0, 80)))
    g_qkv, g_proj, g_up, g_down, g_small = reduce_grads(
        wide_grad, grad_w_down.astype(BF16), small_grad
    )
    g_small = g_small[0]
    return (
        block_out, input_grad, g_small[0:4], g_small[4:8], g_small[8:12], g_small[12:16],
        g_qkv, g_small[16:24], g_small[24:28], g_proj, g_small[28:32], g_up, g_small[32:48],
        g_down,
    )


def solution(mesh):
    both = ("dp", "ctx")
    rows, vec, mat = P("dp", "ctx", None), P(both), P(both, None)
    return jax.shard_map(
        per_device,
        mesh=mesh,
        in_specs=(
            rows, P("dp", "ctx"), P(), vec, vec, vec, vec, mat, vec, mat, vec, mat, vec, mat, rows,
        ),
        out_specs=(
            rows, rows, vec, vec, vec, vec, mat, vec, vec, mat, vec, mat, vec, mat,
        ),
        check_vma=False,
    )
```

time: 1660 us -> 187 us (0.11)
  waiting for transfers between devices: 1190 us -> 0 us
  blocking collectives: 313 us -> 0 us
  Pallas kernels: 0 us -> 134 us
  local copies, waits for them, and re-layouts: 62.9 us -> 20.8 us
  matrix products: 49.5 us -> 21.8 us
    reduce_scatter x3 -> x0, waiting for transfers between devices: 770 us -> none  [the longest x1 635 us: per_device(): lax.psum_scatter(grad_w_down, ('dp', 'ctx'), scatter_dimension=0, tiled=T...]
    all_gather x5 -> x0, waiting for transfers between devices: 339 us -> none  [the longest x1 188 us: per_device(): lax.all_gather(down_weight, ('dp', 'ctx'), axis=0, tiled=True)]
    all_gather x1 -> x0, blocking collectives: 177 us -> none  [per_device(): lax.all_gather(attn_out_weight, ('dp', 'ctx'), axis=0, tiled=True)]
    unnamed x2 -> x0, blocking collectives: 136 us -> none
    pallas_call x0 -> x5, Pallas kernels: none -> 134 us  [the longest x1 48.2 us: gather_weights(): pl.pallas_call(gather_kernel, out_shape=(jax.ShapeDtypeStruct((512, 4096)...]
    unnamed x10 -> x0, waiting for transfers between devices: 83.8 us -> none
    dot_general x40 -> x12, matrix products: 49.5 us -> 21.8 us  [the longest x4 12 us: nn(): lax.dot_general(a, b, (((1,), (0,)), ((), ())), preferred_element_type=F32)]
    dynamic_slice x28 -> x0, local copies, waits for them, and re-layouts: 25.1 us -> none  [the longest x12 13.8 us: scores_for(): lax.dynamic_slice_in_dim(key_src, start, key_rows, 0)]
  transfers between devices with their start and end apart: 9 -> 0, of which waited for: 7 -> 0; matrix products, arithmetic and copies ran while one was open for 7% -> 0% of each run, Pallas kernels for 0% -> 0%
where the time goes in v1:
time: 187 us
  Pallas kernels  134 us (72%)
  matrix products  21.8 us (12%)
  local copies, waits for them, and re-layouts  20.8 us (11%)
  other arithmetic  8.82 us (5%)
    pallas_call x1, Pallas kernels, gather_weights(): pl.pallas_call(gather_kernel, out_shape=(jax.ShapeDtypeStruct((512, 4096)...  48.2 us
    pallas_call x1, Pallas kernels, reduce_grads(): pl.pallas_call(reduce_kernel, out_shape=(jax.ShapeDtypeStruct((4, 1536),...  44.5 us
    pallas_call x1, Pallas kernels, spread_heads(): pl.pallas_call(spread_kernel, out_shape=jax.ShapeDtypeStruct((2, 8, 128,...  16 us
    pallas_call x1, Pallas kernels, collect_heads(): pl.pallas_call(collect_kernel, out_shape=jax.ShapeDtypeStruct((8, 128, 25...  15.4 us
    dot_general x4, matrix products, nn(): lax.dot_general(a, b, (((1,), (0,)), ((), ())), preferred_element_type=F32)  12 us
    pallas_call x1, Pallas kernels, attend(): pl.pallas_call(attend_kernel, out_shape=jax.ShapeDtypeStruct((2, 8, 128,...  9.85 us
    dot_general x4, matrix products, nt(): lax.dot_general(a, b, (((1,), (1,)), ((), ())), preferred_element_type=F32)  5.98 us
    unnamed x42, local copies, waits for them, and re-layouts  5.48 us

profile of v1, /device:TPU:1, one launch (start us, length us, event | category | flops | bytes accessed | tf_op | source)
XLA Modules:
  0.0 186.6 jit_solution(17618583619664306609)
XLA Ops:
  0.6 1.4 pad_maximum_fusion.1.wa_ref
  2.0 0.8 concatenate.90
  2.9 0.6 pad_convert_fusion.sm_ref
  3.5 48.2 %shard_map.254 = (bf16[512,4096]{1,0:T(8,128)(2,1)}, bf16[2048,512]{1,0:T(8,128)(2,1)}, f32[128,8,128]{2,1,0:T(8,128)}) custom-call(bf16[4,4096]{1,0:T(4,128)(2,1)} %pad_maximum_fusion.1.wa_ref, bf16[16,512]{1,0:T(8,128)(2,1)} %wd_ref.1, f32[8,128]{1,0:T(8,128)} %pad_convert_fusion.sm_ref), custom_call_target="tpu_custom_call" | custom-call | tf_op jit(solution)/shard_map/pallas_call | solution.py:164
  51.6 1.4 convolution_convert_fusion.4
  53.0 1.1 slice.157
  54.2 0.1 add.107
  54.3 0.7 fusion.81
  55.1 0.1 mul.224
  55.2 1.0 convert_reduce_fusion.2
  56.3 1.1 fusion.35
  57.4 1.9 %convolution_add_fusion = f32[128,1536]{1,0:T(8,128)S(1)} fusion(bf16[512,4096]{1,0:T(8,128)(2,1)} %get-tuple-element.23, f32[1536]{0:T(1024)S(1)} %add.107, bf16[1,128,512]{2,1,0:T(8,128)(2,1)} %param.15, f32[512]{0:T(512)S(1)} %add.104, f32[512]{0:T(512)S(1)} %mul.224, f32[128]{0:T(128)S(1)} %fusion.71, f32[128]{0:T(128)S(1)} %broadcast_multiply_fusion.1), kind=kOutput, calls=%fused_computation.4 | convolution fusion | flops 201916416 | bytes 2501632 | tf_op jit(solution)/shard_map/dot_general | solution.py:419
  59.3 0.3 copy.58
  60.1 1.0 copy.60.x_ref
  61.1 16.0 %shard_map.255.y_ref = bf16[2,8,128,256]{3,2,1,0:T(8,128)(2,1)} custom-call(bf16[8,128,256]{2,1,0:T(8,128)(2,1)} %copy.60.x_ref), custom_call_target="tpu_custom_call" | custom-call | tf_op jit(solution)/shard_map/pallas_call | solution.py:354
  77.1 9.8 %shard_map.256.z_ref = bf16[2,8,128,256]{3,2,1,0:T(8,128)(2,1)} custom-call(s32[32]{0:T(128)} %order_ref.1, bf16[2,8,128,256]{3,2,1,0:T(8,128)(2,1)} %shard_map.255.y_ref), custom_call_target="tpu_custom_call" | custom-call | tf_op jit(solution)/shard_map/pallas_call | solution.py:468
  86.9 15.4 %shard_map.257 = bf16[8,128,256]{2,1,0:T(8,128)(2,1)} custom-call(bf16[2,8,128,256]{3,2,1,0:T(8,128)(2,1)} %shard_map.256.z_ref), custom_call_target="tpu_custom_call" | custom-call | tf_op jit(solution)/shard_map/pallas_call | solution.py:399
  102.4 1.3 copy.61
  103.7 0.7 fusion.48
  104.4 2.0 %convolution_add_fusion.3 = f32[128,512]{1,0:T(8,128)} fusion(bf16[128,512]{0,1:T(8,128)(2,1)S(1)} %bitcast.178, bf16[512,4096]{1,0:T(8,128)(2,1)} %get-tuple-element.23, bf16[1,128,512]{2,1,0:T(8,128)(2,1)S(1)} %copy-done), kind=kOutput, calls=%fused_computation.17 | convolution fusion | flops 67239936 | bytes 1048576 | tf_op jit(solution)/shard_map/dot_general | solution.py:419
  106.5 0.7 add.116
  107.2 0.7 add.113
  107.9 0.7 mul.236
  108.6 5.9 %multiply_convert_fusion = (bf16[128,2048]{1,0:T(8,128)(2,1)S(1)}, f32[128,2048]{1,0:T(8,128)}, f32[128,2048]{1,0:T(8,128)}) fusion(f32[2048]{0:T(1024)} %add.116, bf16[512,4096]{1,0:T(8,128)(2,1)} %get-tuple-element.23, bf16[1,128,512]{2,1,0:T(8,128)(2,1)S(1)} %copy-done, f32[512]{0:T(512)} %add.113, f32[512]{0:T(512)} %mul.236, f32[128]{0:T(128)} %copy-done.14, ...), kind=kOutput, calls=%fused_computation.24 | convolution fusion | flops 286130176 | bytes 4862976 | tf_op jit(solution)/shard_map/dot_general | solution.py:419
  114.5 1.5 add.120
  116.0 2.2 %fusion.8 = bf16[1,128,512]{2,1,0:T(8,128)(2,1)} fusion(f32[128,512]{1,0:T(8,128)} %convolution_add_fusion.3, bf16[128,2048]{1,0:T(8,128)(2,1)S(1)} %get-tuple-element.44, bf16[2048,512]{1,0:T(8,128)(2,1)S(1)} %copy-done.1, f32[512]{0:T(512)} %add.120), kind=kOutput, calls=%fused_computation.20 | convolution fusion | flops 268632064 | bytes 3016704 | tf_op jit(solution)/shard_map/dot_general | solution.py:419
  118.2 3.0 %convert_reduce_fusion = (f32[2048]{0:T(1024)}, bf16[128,2048]{1,0:T(8,128)(2,1)S(1)}) fusion(f32[128,2048]{1,0:T(8,128)} %get-tuple-element.45, f32[128,2048]{1,0:T(8,128)} %get-tuple-element.83, bf16[2048,512]{1,0:T(8,128)(2,1)S(1)} %copy-done.1, bf16[1,128,512]{2,1,0:T(8,128)(2,1)S(1)} %copy-done.2), kind=kOutput, calls=%fused_computation.22 | convolution fusion | flops 272627712 | bytes 4857856 | tf_op jit(solution)/shard_map/dot_general | solution.py:415
  121.3 0.8 fusion
  122.3 0.3 convert_reduce_fusion.1
  122.6 0.8 fusion.77
  123.4 0.3 fusion.34
  123.8 0.9 convert_reduce_fusion.3
  124.7 0.8 convolution_convert_fusion.1
  125.5 0.3 convolution_convert_fusion.3
  125.8 0.7 convolution_convert_fusion.2
  126.6 2.2 %pad_maximum_fusion.wa_ref = bf16[512,4096]{1,0:T(8,128)(2,1)} fusion(bf16[512,2048]{1,0:T(8,128)(2,1)S(1)} %convolution_convert_fusion.1, bf16[512,512]{1,0:T(8,128)(2,1)S(1)} %convolution_convert_fusion.3, bf16[512,1536]{1,0:T(8,128)(2,1)S(1)} %convolution_convert_fusion.2), kind=kLoop, calls=%fused_computation | loop fusion | flops 12582912 | bytes 8388608 | tf_op jit(solution)/shard_map/concatenate | solution.py:568
  128.7 2.0 %convolution_convert_fusion.wd_ref = bf16[2048,512]{1,0:T(8,128)(2,1)} fusion(bf16[128,2048]{1,0:T(8,128)(2,1)S(1)} %get-tuple-element.44, bf16[1,128,512]{2,1,0:T(8,128)(2,1)S(1)} %copy-done.2), kind=kOutput, calls=%fused_computation.1 | convolution fusion | flops 269484032 | bytes 2752512 | tf_op jit(solution)/shard_map/dot_general | solution.py:423
  131.1 0.1 reshape.420
  131.6 0.2 concatenate.101
  131.8 0.8 pad.44.sm_ref
  132.7 44.5 %shard_map.258 = (f32[4,1536]{1,0:T(4,128)}, f32[4,512]{1,0:T(4,128)}, f32[4,2048]{1,0:T(4,128)}, f32[16,512]{1,0:T(8,128)}, f32[8,128]{1,0:T(8,128)}) custom-call(bf16[512,4096]{1,0:T(8,128)(2,1)} %pad_maximum_fusion.wa_ref, bf16[2048,512]{1,0:T(8,128)(2,1)} %convolution_convert_fusion.wd_ref, f32[128,8,128]{2,1,0:T(8,128)} %pad.44.sm_ref), custom_call_target="tpu_custom_call" | custom-call | tf_op jit(solution)/shard_map/pallas_call | solution.py:284
  177.2 1.5 slice_bitcast_fusion.6
  178.7 1.3 slice_bitcast_fusion.8
  179.9 1.3 slice_bitcast_fusion.5
  181.2 1.3 copy.71
  182.5 1.3 copy.72
  183.8 1.4 copy.73
  185.2 1.4 copy.74
  (76 shorter events, 1.6 us)
Async XLA Ops:
  51.6 8.2 %copy-start.18 = (s32[1,128]{1,0:T(1,128)S(1)}, s32[1,128]{1,0:T(1,128)}, u32[]{:S(2)}) copy-start(s32[1,128]{1,0:T(1,128)} %param.16) | copy-start | bytes 1540
  55.1 2.3 %copy-start.12 = (f32[512]{0:T(512)}, f32[512]{0:T(512)S(1)}, u32[]{:S(2)}) copy-start(f32[512]{0:T(512)S(1)} %add.104) | copy-start | bytes 6148
  55.2 4.8 %copy-start.6 = (f32[512]{0:T(512)}, f32[512]{0:T(512)S(1)}, u32[]{:S(2)}) copy-start(f32[512]{0:T(512)S(1)} %mul.224) | copy-start | bytes 6148
  56.3 3.5 %copy-start.8 = (f32[128]{0:T(128)}, f32[128]{0:T(128)S(1)}, u32[]{:S(2)}) copy-start(f32[128]{0:T(128)S(1)} %broadcast_multiply_fusion.1) | copy-start | bytes 1540
  57.4 2.7 %copy-start.16 = (f32[128]{0:T(128)}, f32[128]{0:T(128)S(1)}, u32[]{:S(2)}) copy-start(f32[128]{0:T(128)S(1)} %fusion.35) | copy-start | bytes 1540
  57.4 2.7 %copy-start.14 = (f32[128]{0:T(128)}, f32[128]{0:T(128)S(1)}, u32[]{:S(2)}) copy-start(f32[128]{0:T(128)S(1)} %fusion.71) | copy-start | bytes 1540
  61.1 43.4 %copy-start = (bf16[1,128,512]{2,1,0:T(8,128)(2,1)S(1)}, bf16[1,128,512]{2,1,0:T(8,128)(2,1)}, u32[]{:S(2)}) copy-start(bf16[1,128,512]{2,1,0:T(8,128)(2,1)} %param.15) | copy-start | bytes 393220
  108.6 7.4 %copy-start.1 = (bf16[2048,512]{1,0:T(8,128)(2,1)S(1)}, bf16[2048,512]{1,0:T(8,128)(2,1)}, u32[]{:S(2)}) copy-start(bf16[2048,512]{1,0:T(8,128)(2,1)} %get-tuple-element.24) | copy-start | bytes 6291460
  108.6 9.6 %copy-start.2 = (bf16[1,128,512]{2,1,0:T(8,128)(2,1)S(1)}, bf16[1,128,512]{2,1,0:T(8,128)(2,1)}, u32[]{:S(2)}) copy-start(bf16[1,128,512]{2,1,0:T(8,128)(2,1)} %param.29) | copy-start | bytes 393220
  116.0 5.3 %copy-start.4 = (bf16[512,4096]{1,0:T(8,128)(2,1)S(1)}, bf16[512,4096]{1,0:T(8,128)(2,1)}, u32[]{:S(2)}) copy-start(bf16[512,4096]{1,0:T(8,128)(2,1)} %get-tuple-element.23) | copy-start | bytes 12582916
  121.2 1.1 copy-start.3
  121.2 1.4 copy-start.5
  121.2 1.4 copy-start.7
  121.2 1.4 copy-start.9
  121.3 2.1 %copy-start.17 = (f32[128]{0:T(128)S(1)}, f32[128]{0:T(128)}, u32[]{:S(2)}) copy-start(f32[128]{0:T(128)} %copy-done.16) | copy-start | bytes 1540
  121.3 2.2 %copy-start.15 = (f32[128]{0:T(128)S(1)}, f32[128]{0:T(128)}, u32[]{:S(2)}) copy-start(f32[128]{0:T(128)} %copy-done.14) | copy-start | bytes 1540
  122.1 2.6 %copy-start.10 = (f32[512]{0:T(512)S(1)}, f32[512]{0:T(512)}, u32[]{:S(2)}) copy-start(f32[512]{0:T(512)} %add.113) | copy-start | bytes 6148
  122.6 3.2 %copy-start.13 = (f32[512]{0:T(512)S(1)}, f32[512]{0:T(512)}, u32[]{:S(2)}) copy-start(f32[512]{0:T(512)} %copy-done.12) | copy-start | bytes 6148
  126.5 5.0 %copy-start.11 = (f32[2048]{0:T(1024)S(1)}, f32[2048]{0:T(1024)}, u32[]{:S(2)}) copy-start(f32[2048]{0:T(1024)} %get-tuple-element.85) | copy-start | bytes 24580

commit v2 on v0

v2 whole, which is shorter than its diff:
```python
import jax
import jax.numpy as jnp
import numpy as np
from jax import lax
from jax.experimental import pallas as pl
from jax.experimental.pallas import tpu as pltpu
from jax.sharding import PartitionSpec as P

EPS = 1e-05
MESH = pl.DeviceIdType.MESH
F32 = jnp.float32
BF16 = jnp.bfloat16
VMEM = pltpu.VMEM
LIMIT = 60 * 1024 * 1024

ORDERS = ((0, 1, 2), (1, 2, 0), (2, 0, 1))
ORDER_OF = (0, 1, 2, 1, 0, 1, 1, 2)
COLS = (256, 128, 128, 128, 256, 256, 128, 384)
LEFT = (0, 256, 384, 0, 512, 768, 0, 128)
N = 8
FIRST, SMALL, LATER = (0, 1, 2), 3, (4, 5, 6, 7)
TILES = [((8, 128), F32) if p == SMALL else ((16, COLS[p]), BF16) for p in range(N)]
SECTIONS_IN = ((4, 0), (4, 4), (4, 8), (4, 12), (12, 16), (4, 28), (16, 32))
SECTIONS_OUT = ((4, 0), (4, 4), (4, 8), (4, 12), (8, 16), (4, 24), (4, 28), (16, 32))


def device_of(x, y, z, core):
    return (z * 2 + lax.rem(x, 2), y * 4 + lax.div(x, 2) * 2 + core)


def slot_of(p, at):
    return sum(at[axis] * 4**k for k, axis in enumerate(ORDERS[ORDER_OF[p]]))


def moved(at, axis, delta):
    at = list(at)
    at[axis] = lax.rem(at[axis] + delta, 4)
    return at


def send(src, dst, ssem, rsem, peer):
    copy = pltpu.make_async_remote_copy(
        src_ref=src, dst_ref=dst, send_sem=ssem, recv_sem=rsem, device_id=peer, device_id_type=MESH
    )
    copy.start()
    return copy


def nt(a, b):
    return lax.dot_general(a, b, (((1,), (1,)), ((), ())), preferred_element_type=F32)


def nn(a, b):
    return lax.dot_general(a, b, (((1,), (0,)), ((), ())), preferred_element_type=F32)


def tn(a, b):
    return lax.dot_general(a, b, (((0,), (0,)), ((), ())), preferred_element_type=F32)


def selectors(n, off):
    cols = lax.broadcasted_iota(jnp.int32, (1, 128 * n), 1)
    owner = ((cols.astype(F32) + 0.5) * (1.0 / n)).astype(jnp.int32)
    lane = cols - owner * n + off
    rows = lax.broadcasted_iota(jnp.int32, (128, 128 * n), 0)
    pick = jnp.where(rows == lane, 1.0, 0.0).astype(BF16)
    return pick, rows == owner


def swap_halves(u):
    lane = lax.broadcasted_iota(jnp.int32, u.shape, 1)
    lane = lane - 64 * (lane >= 64).astype(jnp.int32)
    return jnp.where(lane < 8, pltpu.roll(u, 120, 1), pltpu.roll(u, 8, 1))


def block_kernel(
    table, hid, dy_ref, pos, freq, small, w_qkv, w_proj, w_upper, w_lower,
    out_ref, ingrad_ref, gqkv_ref, gproj_ref, gup_ref, gdown_ref, gsmall_ref,
    *rest,
):
    rest = list(rest)

    def take(count):
        got = rest[:count]
        del rest[:count]
        return got

    bufs, grads, recv = take(N), take(N), take(N)
    squad, rquad, squad2, rquad2, asm, asm2 = take(6)
    wa, wu, wd, ga, gu, gd, smat, gmat = take(8)
    xs, ys, zs, crecv, ctotal, back = take(6)
    qb, kb, vb, db, att_b, dq_b, dk_b, dv_b = take(8)
    xhat, inv_s, cos_s, sin_s, vecs, gvec, h1_s, h2_s, g_s, dup_s, mlp_s, dh2_s, dqkv_s = take(13)
    qs, qr, q2s, q2r, ags, agr, fws, fwr, rss, rsr, sps, spr, sfs, sfr = take(14)
    cos_, cor_, cfs, cfr = take(4)

    dp, ctx = lax.axis_index("dp"), lax.axis_index("ctx")
    core = lax.rem(ctx, 2)
    at = [
        lax.rem(lax.div(ctx, 2), 2) * 2 + lax.rem(dp, 2), lax.div(ctx, 4), lax.div(dp, 2)
    ]
    sibling = device_of(*at, 1 - core)
    q = lax.rem(ctx, 4)
    axis_peers = [
        [device_of(*moved(at, axis, delta), core) for delta in (1, 2, 3)] for axis in range(3)
    ]
    far = moved(at, 0, 2)
    far_cross = device_of(*far, 1 - core)
    head_at = []
    for delta in range(8):
        place = moved(far if delta % 2 else at, 1, delta // 2)
        head_at.append((place[1] * 2 + lax.div(place[0], 2), device_of(*place, core)))
    me = head_at[0][0]
    quad_peers = [(sibling, 1), (head_at[1][1], 2), (far_cross, 3)]

    def quad_index(delta):
        core_t = 1 - core if delta % 2 else core
        hi = lax.div(at[0], 2)
        return (1 - hi if delta // 2 else hi) * 2 + core_t

    everyone = [sibling, far_cross] + sum(axis_peers, [])
    everyone += [head_at[delta][1] for delta in (3, 5, 7)]
    barrier = pltpu.get_barrier_semaphore()
    for peer in everyone:
        pl.semaphore_signal(barrier, inc=1, device_id=peer, device_id_type=MESH)

    slots = [slot_of(p, at) for p in range(N)]
    started = []

    squad[...] = jnp.zeros_like(squad)
    qkv_rows = w_qkv[...].astype(F32)
    up_rows = w_upper[...].astype(F32)
    for t in range(3):
        squad[t, 0:4, 0:512] = qkv_rows[:, 512 * t : 512 * (t + 1)]
    squad[3, 0:4, 0:512] = w_proj[...].astype(F32)
    for t in range(4):
        squad[t, 0:4, 512:1024] = up_rows[:, 512 * t : 512 * (t + 1)]
    for p in (6, 7):
        bufs[p][core, slots[p]] = w_lower[:, LEFT[p] : LEFT[p] + COLS[p]]
    bufs[SMALL][core, slots[SMALL]] = small[...]
    pl.semaphore_wait(barrier, len(everyone))

    quad = []
    for peer, delta in quad_peers:
        quad.append(
            send(squad.at[quad_index(delta)], rquad.at[q], qs.at[delta - 1], qr.at[delta - 1], peer)
        )
    started += quad
    rquad[q] = squad[q]
    hops, fwd = {}, {}

    def block(p, k):
        size = 4**k
        return lax.div(slots[p], size) * size, size

    def gather_send(p, k):
        base, size = block(p, k)
        axis = ORDERS[ORDER_OF[p]][k]
        part = bufs[p].at[core, pl.ds(base, size)]
        for d in range(3):
            hops[p, k, d] = send(
                part, part, ags.at[p, 3 * k + d], agr.at[p, 3 * k + d], axis_peers[axis][d]
            )
            started.append(hops[p, k, d])
        if k == 2:
            fwd[p, 3] = send(part, part, fws.at[p, 3], fwr.at[p, 3], sibling)
            started.append(fwd[p, 3])

    def gather_wait(p, k):
        for d in range(3):
            hops[p, k, d].wait_recv()

    def gather_forward(p):
        axis = ORDERS[ORDER_OF[p]][2]
        for d in range(3):
            hops[p, 2, d].wait_recv()
            base = lax.rem(at[axis] + 3 - d, 4) * 16
            part = bufs[p].at[core, pl.ds(base, 16)]
            fwd[p, d] = send(part, part, fws.at[p, d], fwr.at[p, d], sibling)
            started.append(fwd[p, d])

    def gather_done(p):
        for d in range(4):
            fwd[p, d].wait_recv()

    for p in (SMALL, 6, 7):
        gather_send(p, 0)
    for copy in quad:
        copy.wait_recv()
    for t in range(4):
        asm[4 * t : 4 * t + 4, :] = rquad[t, 0:4, :]
    for p in (0, 1, 2, 4, 5):
        bufs[p][core, slots[p]] = asm[:, LEFT[p] : LEFT[p] + COLS[p]].astype(BF16)
        gather_send(p, 0)

    x = hid[0].astype(F32)
    center = x - jnp.mean(x, axis=1, keepdims=True)
    inv = lax.rsqrt(jnp.mean(center * center, axis=1, keepdims=True) + EPS)
    xhat[...] = center * inv
    inv_s[...] = jnp.broadcast_to(inv, (128, 128))
    places = jnp.transpose(jnp.broadcast_to(pos[...].astype(F32), (128, 128)))
    angle = places * freq[...]
    lane = lax.broadcasted_iota(jnp.int32, (128, 128), 1)
    lane = lane - 64 * (lane >= 64).astype(jnp.int32)
    sine = jnp.sin(angle)
    cos_s[...] = jnp.cos(angle)
    sin_s[...] = jnp.where(lane < 8, -sine, sine)

    for k in (1, 2):
        for p in (SMALL,) + FIRST + LATER:
            gather_wait(p, k - 1)
            gather_send(p, k)
    for p in (SMALL,) + FIRST:
        gather_forward(p)

    def place_of(row, t):
        x_lo = lax.rem(lax.div(row, 4), 2)
        return [(t // 2) * 2 + x_lo, lax.rem(row, 4), lax.div(row, 8)], t % 2

    def wide_loop(streams, left0, store):
        def body(row, carry):
            rows = pl.ds(pl.multiple_of(row * 16, 16), 16)
            for t in range(4):
                where, c = place_of(row, t)
                for p in streams:
                    left = 512 * t + LEFT[p] - left0
                    store(p, c, slot_of(p, where), rows, left)
            return carry

        lax.fori_loop(0, 32, body, 0)

    def tall_loop(store):
        def body(row, carry):
            for t in range(4):
                where, c = place_of(row, t)
                rows = pl.ds(pl.multiple_of(row * 64 + t * 16, 16), 16)
                for p in (6, 7):
                    store(p, c, slot_of(p, where), rows, LEFT[p])
            return carry

        lax.fori_loop(0, 32, body, 0)

    def unpack_to(dst):
        def store(p, c, slot, rows, left):
            dst[rows, left : left + COLS[p]] = bufs[p][c, slot]

        return store

    def pack_from(src):
        def store(p, c, slot, rows, left):
            grads[p][c, slot] = src[rows, left : left + COLS[p]]

        return store

    gather_done(SMALL)

    def small_rows(row, carry):
        for t in range(4):
            where, c = place_of(row, t)
            smat[pl.ds(row * 4 + t, 1), :] = bufs[SMALL][c, slot_of(SMALL, where), 0:1, :]
        return carry

    lax.fori_loop(0, 32, small_rows, 0)
    tiles = smat[...].astype(BF16)
    for i, (n, off) in enumerate(SECTIONS_IN):
        pick, own = selectors(n, off)
        vecs[i : i + 1, 0 : 128 * n] = jnp.sum(
            jnp.where(own, nn(tiles, pick), 0.0), axis=0, keepdims=True
        )
    normed = xhat[...]
    h1_s[...] = (normed * vecs[0:1, 0:512] + vecs[1:2, 0:512]).astype(BF16)
    h2_s[...] = (normed * vecs[2:3, 0:512] + vecs[3:4, 0:512]).astype(BF16)
    for p in FIRST:
        gather_done(p)
    wide_loop(FIRST, 0, unpack_to(wa))

    dy = dy_ref[0]
    parts = [nn(h1_s[...], wa[:, 512 * i : 512 * (i + 1)]) for i in range(3)]
    parts = [parts[i] + vecs[4:5, 512 * i : 512 * (i + 1)] for i in range(3)]
    cos_t, sin_t = cos_s[...], sin_s[...]

    def turn(u, sign):
        return jnp.concatenate(
            [
                u[:, c : c + 128] * cos_t + swap_halves(u[:, c : c + 128]) * (sin_t * sign)
                for c in range(0, 512, 128)
            ],
            axis=1,
        )

    sent = [turn(parts[0], 1.0), turn(parts[1], 1.0), parts[2], nt(dy, wa[:, 1536:2048])]
    sent = [item.astype(BF16) for item in sent]
    for h in range(8):
        piece = jnp.concatenate([item[:, 64 * h : 64 * h + 64] for item in sent], axis=1)
        xs[h, 0] = piece[0:64]
        xs[h, 1] = piece[64:128]
    spread, spread_fwd = [], []

    def spot(c, m):
        return pl.ds(c * 16 + m * 2, 2)

    for delta in range(1, 8):
        m, peer = head_at[delta]
        spread.append(
            send(xs.at[m], ys.at[spot(core, me)], sps.at[delta - 1], spr.at[delta - 1], peer)
        )
    ys[spot(core, me)] = xs[me]
    mine = ys.at[spot(core, me)]
    spread_fwd.append(send(mine, mine, sfs.at[0], sfr.at[0], sibling))

    for p in LATER:
        gather_forward(p)
    for p in LATER:
        gather_done(p)
    wide_loop((4, 5), 512, unpack_to(wu))
    tall_loop(unpack_to(wd))

    def mlp(t):
        cols = slice(512 * t, 512 * (t + 1))
        up = nn(h2_s[...], wu[:, cols]) + vecs[6:7, cols]
        cdf = 0.5 * (1.0 + lax.erf(up * np.float32(0.5**0.5)))
        pdf = jnp.exp(-0.5 * up * up) * np.float32((2 * np.pi) ** -0.5)
        g = (up * cdf).astype(BF16)
        d_up = (nt(dy, wd[cols, :]) * (cdf + up * pdf)).astype(BF16)
        g_s[:, cols] = g
        dup_s[:, cols] = d_up
        gvec[7:8, cols] = jnp.sum(d_up.astype(F32), axis=0, keepdims=True)
        gu[:, cols] = tn(h2_s[...], d_up).astype(BF16)
        gd[cols, :] = tn(g, dy).astype(BF16)

    for t in range(4):
        mlp(t)
        if t == 1:
            for delta in range(1, 8):
                back_y = (4 - delta // 2) % 4
                m = head_at[back_y * 2 + delta % 2][0]
                spread[delta - 1].wait_recv()
                part = ys.at[spot(core, m)]
                spread_fwd.append(send(part, part, sfs.at[delta], sfr.at[delta], sibling))
    started += spread + spread_fwd

    adds = {}

    def reduce_start(p):
        adds[p, 3] = send(
            grads[p].at[1 - core], recv[p].at[pl.ds(0, 64)], rss.at[p, 9], rsr.at[p, 9], sibling
        )
        started.append(adds[p, 3])

    def offset(k):
        return 64 + {2: 0, 1: 48, 0: 60}[k]

    def reduce_step(p, k):
        if k == 2:
            adds[p, 3].wait_recv()
            total, others, base = 64, (0,), 0
        else:
            for d in range(3):
                adds[p, k + 1, d].wait_recv()
            base, total = block(p, k + 1)
            others = [offset(k + 1) + d * total for d in range(3)]
        unit = min(total, 4)

        def body(i, carry):
            here = pl.ds(base + i * unit, unit)
            value = grads[p][core, here].astype(F32)
            for other in others:
                value = value + recv[p][pl.ds(other + i * unit, unit)].astype(F32)
            grads[p][core, here] = value.astype(grads[p].dtype)
            return carry

        lax.fori_loop(0, total // unit, body, 0)
        axis = ORDERS[ORDER_OF[p]][k]
        size = 4**k
        own, _ = block(p, k)
        for d in range(3):
            there = lax.rem(at[axis] + d + 1, 4)
            part = grads[p].at[core, pl.ds(own + (there - at[axis]) * size, size)]
            adds[p, k, d] = send(
                part, recv[p].at[pl.ds(offset(k) + d * size, size)],
                rss.at[p, 3 * k + d], rsr.at[p, 3 * k + d], axis_peers[axis][d],
            )
            started.append(adds[p, k, d])

    def reduce_end(p):
        for d in range(3):
            adds[p, 0, d].wait_recv()
        value = grads[p][core, slots[p]].astype(F32)
        for d in range(3):
            value = value + recv[p][offset(0) + d].astype(F32)
        return value

    wide_loop((4, 5), 512, pack_from(gu))
    tall_loop(pack_from(gd))
    for p in LATER:
        reduce_start(p)

    for copy in spread_fwd:
        copy.wait_recv()
    for t in range(32):
        part = ys[table[32 + t]]
        rows = slice(64 * t, 64 * t + 64)
        qb[rows, :] = part[:, 0:64]
        kb[rows, :] = part[:, 64:128]
        vb[rows, :] = part[:, 128:192]
        db[rows, :] = part[:, 192:256]
    att_b[...] = jnp.zeros_like(att_b)
    dq_b[...] = jnp.zeros_like(dq_b)
    dk_b[...] = jnp.zeros_like(dk_b)
    dv_b[...] = jnp.zeros_like(dv_b)

    def tile(j):
        width = 512 * (j + 1)
        row = 512 * j + 256 * (1 - core if j % 2 else core)
        rows = pl.ds(pl.multiple_of(row, 256), 256)
        queries = qb[rows, :] * jnp.asarray(0.125, BF16)
        d_o = db[rows, :]
        keys, vals = kb[0:width, :], vb[0:width, :]
        scores = nt(queries, keys)
        at_q = row + lax.broadcasted_iota(jnp.int32, (256, width), 0)
        at_k = lax.broadcasted_iota(jnp.int32, (256, width), 1)
        scores = jnp.where(at_q >= at_k, scores, -1e30)
        probs = jnp.exp(scores - jnp.max(scores, axis=1, keepdims=True))
        probs = probs * (1.0 / jnp.sum(probs, axis=1, keepdims=True))
        low = probs.astype(BF16)
        att = nn(low, vals)
        delta = jnp.sum(d_o.astype(F32) * att, axis=1, keepdims=True)
        d_s = (probs * (nt(d_o, vals) - delta)).astype(BF16)
        blocks = pl.ds(8 * j + 4 * (1 - core if j % 2 else core), 4)
        att_b[blocks] = att.reshape(4, 64, 64)
        dq_b[blocks] = (nn(d_s, keys) * 0.125).reshape(4, 64, 64)
        reach = slice(0, 8 * (j + 1))
        dk_b[reach] += tn(d_s, queries).reshape(8 * (j + 1), 64, 64)
        dv_b[reach] += tn(low, d_o).reshape(8 * (j + 1), 64, 64)

    for j in range(4):
        tile(j)
        if j > 0:
            for p in LATER:
                reduce_step(p, 3 - j)
    for i in range(32):
        t = table[i]
        zs[i] = jnp.concatenate([att_b[t], dq_b[t], dk_b[t], dv_b[t]], axis=1).astype(BF16)

    order = (1, 2, 3, 4, 5, 6, 7, 0)
    halves, collect = {}, []
    for delta in order:
        m, _ = head_at[delta]
        halves[delta] = send(
            zs.at[spot(1 - core, m)], crecv.at[m], cfs.at[delta], cfr.at[delta], sibling
        )
    started += list(halves.values())
    mlp_s[...] = nn(g_s[...], wd[...])
    for delta in order:
        m, peer = head_at[delta]
        halves[delta].wait_recv()
        ctotal[m] = zs[spot(core, m)] + crecv[m]
        if delta:
            collect.append(
                send(ctotal.at[m], back.at[me], cos_.at[delta - 1], cor_.at[delta - 1], peer)
            )
        else:
            back[me] = ctotal[m]
    started += collect
    dh2_s[...] = nt(dup_s[...], wu[...])
    dh2 = dh2_s[...]
    gvec[2:3, 0:512] = jnp.sum(dh2 * xhat[...], axis=0, keepdims=True)
    gvec[3:4, 0:512] = jnp.sum(dh2, axis=0, keepdims=True)
    gvec[6:7, 0:512] = jnp.sum(dy.astype(F32), axis=0, keepdims=True)
    for p in LATER:
        value = reduce_end(p)
        if p < 6:
            asm2[:, LEFT[p] : LEFT[p] + COLS[p]] = value
        else:
            gdown_ref[:, LEFT[p] : LEFT[p] + COLS[p]] = value
    for copy in collect:
        copy.wait_recv()

    def whole(i):
        return jnp.concatenate(
            [
                jnp.concatenate(
                    [back[h, 0, :, 64 * i : 64 * i + 64], back[h, 1, :, 64 * i : 64 * i + 64]],
                    axis=0,
                )
                for h in range(8)
            ],
            axis=1,
        )

    dqkv_s[:, 0:512] = turn(whole(1).astype(F32), -1.0).astype(BF16)
    dqkv_s[:, 512:1024] = turn(whole(2).astype(F32), -1.0).astype(BF16)
    dqkv_s[:, 1024:1536] = whole(3)
    mixed = whole(0)
    ga[:, 1536:2048] = tn(mixed, dy).astype(BF16)
    for t in range(3):
        ga[:, 512 * t : 512 * (t + 1)] = tn(
            h1_s[...], dqkv_s[:, 512 * t : 512 * (t + 1)]
        ).astype(BF16)
    wide_loop(FIRST, 0, pack_from(ga))
    for p in FIRST:
        reduce_start(p)
    dh1 = nt(dqkv_s[...], wa[:, 0:1536])
    gvec[0:1, 0:512] = jnp.sum(dh1 * xhat[...], axis=0, keepdims=True)
    gvec[1:2, 0:512] = jnp.sum(dh1, axis=0, keepdims=True)
    gvec[4:5, 0:1024] = jnp.sum(dqkv_s[:, 0:1024].astype(F32), axis=0, keepdims=True)
    gvec[5:6, 0:512] = jnp.sum(dqkv_s[:, 1024:1536].astype(F32), axis=0, keepdims=True)
    spread_out = jnp.zeros((128, 128), F32)
    for i, (n, off) in enumerate(SECTIONS_OUT):
        pick, own = selectors(n, off)
        value = jnp.where(own, gvec[i : i + 1, 0 : 128 * n], 0.0)
        high = value.astype(BF16)
        low = (value - high.astype(F32)).astype(BF16)
        spread_out = spread_out + nt(high, pick) + nt(low, pick)
    gmat[...] = spread_out
    grads[SMALL][...] = jnp.zeros_like(grads[SMALL])

    def small_grads(row, carry):
        for t in range(4):
            where, c = place_of(row, t)
            grads[SMALL][c, slot_of(SMALL, where), 0:1, :] = gmat[pl.ds(row * 4 + t, 1), :]
        return carry

    lax.fori_loop(0, 32, small_grads, 0)
    reduce_start(SMALL)
    for p in FIRST:
        reduce_step(p, 2)
    reduce_step(SMALL, 2)
    d_norm = dh1 * vecs[0:1, 0:512] + dh2_s[...] * vecs[2:3, 0:512]
    normed = xhat[...]
    d_x = d_norm - jnp.mean(d_norm, axis=1, keepdims=True)
    d_x = d_x - normed * jnp.mean(d_norm * normed, axis=1, keepdims=True)
    ingrad_ref[0] = dy.astype(F32) + d_x * inv_s[:, 0:1]
    result = hid[0].astype(F32) + nn(mixed, wa[:, 1536:2048]) + mlp_s[...] + vecs[5:6, 0:512]
    out_ref[0] = result.astype(BF16)
    for k in (1, 0):
        for p in FIRST + (SMALL,):
            reduce_step(p, k)
    for p in FIRST:
        asm2[:, LEFT[p] : LEFT[p] + COLS[p]] = reduce_end(p)
    gsmall_ref[...] = reduce_end(SMALL)
    squad2[...] = jnp.zeros_like(squad2)
    for t in range(4):
        squad2[t, 0:4, :] = asm2[4 * t : 4 * t + 4, :]
    quad = []
    for peer, delta in quad_peers:
        quad.append(
            send(
                squad2.at[quad_index(delta)], rquad2.at[q], q2s.at[delta - 1], q2r.at[delta - 1],
                peer,
            )
        )
    started += quad
    rquad2[q] = squad2[q]
    for copy in quad:
        copy.wait_recv()
    for t in range(3):
        gqkv_ref[:, 512 * t : 512 * (t + 1)] = rquad2[t, 0:4, 0:512]
    gproj_ref[...] = rquad2[3, 0:4, 0:512]
    for t in range(4):
        gup_ref[:, 512 * t : 512 * (t + 1)] = rquad2[t, 0:4, 512:1024]
    for copy in started:
        copy.wait_send()


def run_block(*args):
    dma = pltpu.SemaphoreType.DMA
    scratch = [VMEM((2, 64) + tile, dtype) for tile, dtype in TILES] * 2
    scratch += [VMEM((128,) + tile, dtype) for tile, dtype in TILES]
    scratch += [VMEM((4, 8, 1024), F32)] * 4 + [VMEM((16, 1024), F32)] * 2
    scratch += [VMEM((512, 2048), BF16), VMEM((512, 2048), BF16), VMEM((2048, 512), BF16)] * 2
    scratch += [VMEM((128, 128), F32)] * 2
    scratch += [VMEM((8, 2, 64, 256), BF16), VMEM((32, 64, 256), BF16), VMEM((32, 64, 256), BF16)]
    scratch += [VMEM((8, 2, 64, 256), BF16)] * 3
    scratch += [VMEM((2048, 64), BF16)] * 4 + [VMEM((32, 64, 64), F32)] * 4
    scratch += [VMEM((128, 512), F32)] + [VMEM((128, 128), F32)] * 3 + [VMEM((8, 2048), F32)] * 2
    scratch += [VMEM((128, 512), BF16)] * 2 + [VMEM((128, 2048), BF16)] * 2
    scratch += [VMEM((128, 512), F32)] * 2 + [VMEM((128, 1536), BF16)]
    scratch += [dma((3,))] * 4 + [dma((N, 9))] * 2 + [dma((N, 4))] * 2 + [dma((N, 10))] * 2
    scratch += [dma((7,)), dma((7,)), dma((8,)), dma((8,))] * 2
    shape = jax.ShapeDtypeStruct
    return pl.pallas_call(
        block_kernel,
        out_shape=(
            shape((1, 128, 512), BF16), shape((1, 128, 512), F32), shape((4, 1536), F32),
            shape((4, 512), F32), shape((4, 2048), F32), shape((16, 512), F32), shape((8, 128), F32),
        ),
        in_specs=[pl.BlockSpec(memory_space=pltpu.SMEM)] + [pl.BlockSpec(memory_space=VMEM)] * 9,
        out_specs=[pl.BlockSpec(memory_space=VMEM)] * 7,
        scratch_shapes=scratch,
        compiler_params=pltpu.CompilerParams(
            collective_id=0, has_side_effects=True, vmem_limit_bytes=LIMIT
        ),
    )(*args)


def finish_kernel(*refs):
    for src, dst in zip(refs[:6], refs[7:13]):
        dst[...] = src[...]
    row = refs[6][0:1, :]
    for (n, off), dst in zip(SECTIONS_OUT, refs[13:]):
        dst[...] = row[:, off : off + n]


def finish(*parts):
    shape = jax.ShapeDtypeStruct
    return pl.pallas_call(
        finish_kernel,
        out_shape=tuple(shape(part.shape, part.dtype) for part in parts[:6])
        + tuple(shape((1, n), F32) for n, _ in SECTIONS_OUT),
        in_specs=[pl.BlockSpec(memory_space=VMEM)] * 7,
        out_specs=[pl.BlockSpec(memory_space=VMEM)] * 14,
    )(*parts)


def per_device(
    hidden_in, positions, block_order, norm1_gain, norm1_bias, norm2_gain, norm2_bias,
    qkv_weight, qkv_bias, attn_out_weight, out_bias, up_weight, up_bias, down_weight, out_grad,
):
    small = jnp.concatenate(
        [norm1_gain, norm1_bias, norm2_gain, norm2_bias, qkv_bias, out_bias, up_bias]
    ).astype(F32)
    small = jnp.pad(small[None], ((0, 7), (0, 80)))
    held = block_order.reshape(8, 2, 2).transpose(1, 0, 2).reshape(32)
    ids = jnp.arange(32, dtype=jnp.int32)
    inverse = jnp.sum(jnp.where(held[:, None] == ids[None, :], ids[:, None], 0), axis=0)
    table = jnp.concatenate([held, inverse])
    freqs = 10000.0 ** (-np.arange(8, dtype=np.float32) * np.float32(2.0) / np.float32(16))
    lanes = np.concatenate([freqs, freqs, np.zeros(48)]).astype(np.float32)
    freq = jnp.asarray(np.concatenate([lanes, lanes])[None])
    parts = run_block(
        table, hidden_in, out_grad, positions, freq, small,
        qkv_weight, attn_out_weight, up_weight, down_weight,
    )
    done = finish(*parts)
    block_out, input_grad, g_qkv, g_proj, g_up, g_down = done[:6]
    n1g, n1b, n2g, n2b, qk, val, out, up = (item.reshape(-1) for item in done[6:])
    return (
        block_out, input_grad, n1g, n1b, n2g, n2b, g_qkv, qk, val, g_proj, out, g_up, up, g_down,
    )


def solution(mesh):
    both = ("dp", "ctx")
    rows, vec, mat = P("dp", "ctx", None), P(both), P(both, None)
    return jax.shard_map(
        per_device,
        mesh=mesh,
        in_specs=(
            rows, P("dp", "ctx"), P(), vec, vec, vec, vec, mat, vec, mat, vec, mat, vec, mat, rows,
        ),
        out_specs=(
            rows, rows, vec, vec, vec, vec, mat, vec, vec, mat, vec, mat, vec, mat,
        ),
        check_vma=False,
    )
```

time: 1660 us -> 111 us (0.07)
  waiting for transfers between devices: 1190 us -> 0 us
  blocking collectives: 313 us -> 0 us
  Pallas kernels: 0 us -> 108 us
  local copies, waits for them, and re-layouts: 62.9 us -> 1.03 us
  matrix products: 49.5 us -> 0 us
    reduce_scatter x3 -> x0, waiting for transfers between devices: 770 us -> none  [the longest x1 635 us: per_device(): lax.psum_scatter(grad_w_down, ('dp', 'ctx'), scatter_dimension=0, tiled=T...]
    all_gather x5 -> x0, waiting for transfers between devices: 339 us -> none  [the longest x1 188 us: per_device(): lax.all_gather(down_weight, ('dp', 'ctx'), axis=0, tiled=True)]
    all_gather x1 -> x0, blocking collectives: 177 us -> none  [per_device(): lax.all_gather(attn_out_weight, ('dp', 'ctx'), axis=0, tiled=True)]
    unnamed x2 -> x0, blocking collectives: 136 us -> none
    pallas_call x0 -> x2, Pallas kernels: none -> 108 us  [the longest x1 106 us: run_block(): pl.pallas_call(block_kernel, out_shape=(shape((1, 128, 512), BF16), shape...]
    unnamed x10 -> x0, waiting for transfers between devices: 83.8 us -> none
    dot_general x40 -> x0, matrix products: 49.5 us -> none  [the longest x4 9.74 us: cross_rows(): lax.dot_general(left, right, (((0,), (0,)), ((), ())), preferred_element_...]
    dynamic_slice x28 -> x0, local copies, waits for them, and re-layouts: 25.1 us -> none  [the longest x12 13.8 us: scores_for(): lax.dynamic_slice_in_dim(key_src, start, key_rows, 0)]
  transfers between devices with their start and end apart: 9 -> 0, of which waited for: 7 -> 0; matrix products, arithmetic and copies ran while one was open for 7% -> 0% of each run, Pallas kernels for 0% -> 0%
where the time goes in v2:
time: 111 us
  Pallas kernels  108 us (97%)
  other arithmetic  1.28 us (1%)
    pallas_call x1, Pallas kernels, run_block(): pl.pallas_call(block_kernel, out_shape=(shape((1, 128, 512), BF16), shape...  106 us

profile of v2, /device:TPU:1, one launch (start us, length us, event | category | flops | bytes accessed | tf_op | source)
XLA Modules:
  0.0 111.1 jit_solution(7507086089965701766)
XLA Ops:
  0.6 0.0 copy-start.4
  0.7 0.0 copy-start.5
  0.7 0.0 copy-start.6
  0.7 0.0 copy-start.7
  0.7 0.0 copy-start.1
  0.7 0.0 copy-start.2
  0.7 0.0 copy-start.3
  0.7 0.6 copy-done.4
  1.3 0.0 copy-done.5
  1.3 0.0 copy-done.6
  1.3 0.0 copy-done.7
  1.4 0.0 copy-done.1
  1.4 0.0 copy-done.2
  1.4 0.0 copy-done.3
  1.4 0.1 concatenate.35
  1.5 0.0 copy-start
  1.5 0.6 pad_convert_fusion.small
  2.1 0.1 copy-done
  2.2 0.1 reshape.153
  2.3 0.1 reshape.154
  2.4 0.1 select_reduce_fusion
  2.4 0.6 pad_add_fusion.table
  3.0 106.1 %shard_map.263 = (bf16[1,128,512]{2,1,0:T(8,128)(2,1)}, f32[1,128,512]{2,1,0:T(8,128)}, f32[4,1536]{1,0:T(4,128)}, f32[4,512]{1,0:T(4,128)}, f32[4,2048]{1,0:T(4...) custom-call(s32[64]{0:T(128)} %pad_add_fusion.table, bf16[1,128,512]{2,1,0:T(8,128)(2,1)} %hid.1, ...), custom_call_target="tpu_custom_call" | custom-call | tf_op jit(solution)/shard_map/pallas_call | solution.py:582
  109.1 1.8 %shard_map.264 = (bf16[1,128,512]{2,1,0:T(8,128)(2,1)}, f32[1,128,512]{2,1,0:T(8,128)}, f32[4,1536]{1,0:T(4,128)}, f32[4,512]{1,0:T(4,128)}, f32[4,2048]{1,0:T(4...) custom-call(bf16[1,128,512]{2,1,0:T(8,128)(2,1)} %get-tuple-element., ...), custom_call_target="tpu_custom_call" | custom-call | tf_op jit(solution)/shard_map/pallas_call | solution.py:607
  (1 shorter events, 0.0 us)
Async XLA Ops:
  0.6 0.7 copy-start.4
  0.7 0.7 copy-start.5
  0.7 0.7 copy-start.6
  0.7 0.7 copy-start.7
  0.7 0.7 copy-start.1
  0.7 0.7 copy-start.2
  0.7 0.7 copy-start.3
  1.5 0.7 copy-start

commit v3 on v2

--- a/solution.py
+++ b/solution.py
@@ -64,7 +64,7 @@
     lane = cols - owner * n + off
     rows = lax.broadcasted_iota(jnp.int32, (128, 128 * n), 0)
     pick = jnp.where(rows == lane, 1.0, 0.0).astype(BF16)
-    return pick, rows == owner
+    return pick, jnp.where(rows == owner, 1.0, 0.0).astype(BF16)
 
 
 def swap_halves(u):
@@ -93,6 +93,7 @@
     xhat, inv_s, cos_s, sin_s, vecs, gvec, h1_s, h2_s, g_s, dup_s, mlp_s, dh2_s, dqkv_s = take(13)
     qs, qr, q2s, q2r, ags, agr, fws, fwr, rss, rsr, sps, spr, sfs, sfr = take(14)
     cos_, cor_, cfs, cfr = take(4)
+    pick_in, own_in, pick_out, own_out, kt_b, vt_b = take(6)
 
     dp, ctx = lax.axis_index("dp"), lax.axis_index("ctx")
     core = lax.rem(ctx, 2)
@@ -205,13 +206,27 @@
     sine = jnp.sin(angle)
     cos_s[...] = jnp.cos(angle)
     sin_s[...] = jnp.where(lane < 8, -sine, sine)
-
-    for k in (1, 2):
-        for p in (SMALL,) + FIRST + LATER:
-            gather_wait(p, k - 1)
-            gather_send(p, k)
+    for sections, picks, owns in (
+        (SECTIONS_IN, pick_in, own_in), (SECTIONS_OUT, pick_out, own_out)
+    ):
+        left = 0
+        for n, off in sections:
+            pick, own = selectors(n, off)
+            picks[:, left : left + 128 * n] = pick
+            owns[:, left : left + 128 * n] = own
+            left += 128 * n
+
+    for p in (SMALL,) + FIRST + LATER:
+        gather_wait(p, 0)
+        gather_send(p, 1)
+    for p in (SMALL,) + FIRST:
+        gather_wait(p, 1)
+        gather_send(p, 2)
     for p in (SMALL,) + FIRST:
         gather_forward(p)
+    for p in LATER:
+        gather_wait(p, 1)
+        gather_send(p, 2)
 
     def place_of(row, t):
         x_lo = lax.rem(lax.div(row, 4), 2)
@@ -262,10 +277,12 @@
 
     lax.fori_loop(0, 32, small_rows, 0)
     tiles = smat[...].astype(BF16)
+    left = 0
     for i, (n, off) in enumerate(SECTIONS_IN):
-        pick, own = selectors(n, off)
+        cols = slice(left, left + 128 * n)
+        left += 128 * n
         vecs[i : i + 1, 0 : 128 * n] = jnp.sum(
-            jnp.where(own, nn(tiles, pick), 0.0), axis=0, keepdims=True
+            own_in[:, cols].astype(F32) * nn(tiles, pick_in[:, cols]), axis=0, keepdims=True
         )
     normed = xhat[...]
     h1_s[...] = (normed * vecs[0:1, 0:512] + vecs[1:2, 0:512]).astype(BF16)
@@ -397,47 +414,68 @@
 
     for copy in spread_fwd:
         copy.wait_recv()
+    ones = jnp.where(lax.broadcasted_iota(jnp.int32, (64, 64), 1) < 2, 1.0, 0.0).astype(BF16)
     for t in range(32):
         part = ys[table[32 + t]]
         rows = slice(64 * t, 64 * t + 64)
         qb[rows, :] = part[:, 0:64]
         kb[rows, :] = part[:, 64:128]
-        vb[rows, :] = part[:, 128:192]
+        vb[rows, :] = jnp.concatenate([part[:, 128:192], ones], axis=1)
         db[rows, :] = part[:, 192:256]
-    att_b[...] = jnp.zeros_like(att_b)
-    dq_b[...] = jnp.zeros_like(dq_b)
-    dk_b[...] = jnp.zeros_like(dk_b)
-    dv_b[...] = jnp.zeros_like(dv_b)
+    kt_b[...] = jnp.transpose(kb[...].astype(F32)).astype(BF16)
+    vt_b[...] = jnp.transpose(vb[:, 0:64].astype(F32)).astype(BF16)
 
     def tile(j):
-        width = 512 * (j + 1)
-        row = 512 * j + 256 * (1 - core if j % 2 else core)
+        low, width = 512 * j, 512 * (j + 1)
+        turn_off = 1 - core if j % 2 else core
+        row = low + 256 * turn_off
         rows = pl.ds(pl.multiple_of(row, 256), 256)
-        queries = qb[rows, :] * jnp.asarray(0.125, BF16)
-        d_o = db[rows, :]
-        keys, vals = kb[0:width, :], vb[0:width, :]
-        scores = nt(queries, keys)
-        at_q = row + lax.broadcasted_iota(jnp.int32, (256, width), 0)
-        at_k = lax.broadcasted_iota(jnp.int32, (256, width), 1)
-        scores = jnp.where(at_q >= at_k, scores, -1e30)
-        probs = jnp.exp(scores - jnp.max(scores, axis=1, keepdims=True))
-        probs = probs * (1.0 / jnp.sum(probs, axis=1, keepdims=True))
-        low = probs.astype(BF16)
-        att = nn(low, vals)
-        delta = jnp.sum(d_o.astype(F32) * att, axis=1, keepdims=True)
-        d_s = (probs * (nt(d_o, vals) - delta)).astype(BF16)
-        blocks = pl.ds(8 * j + 4 * (1 - core if j % 2 else core), 4)
-        att_b[blocks] = att.reshape(4, 64, 64)
-        dq_b[blocks] = (nn(d_s, keys) * 0.125).reshape(4, 64, 64)
-        reach = slice(0, 8 * (j + 1))
-        dk_b[reach] += tn(d_s, queries).reshape(8 * (j + 1), 64, 64)
-        dv_b[reach] += tn(low, d_o).reshape(8 * (j + 1), 64, 64)
-
-    for j in range(4):
+        queries = qb[rows, :].astype(F32) * 0.125
+        q_t = jnp.transpose(queries).astype(BF16)
+        do_t = jnp.transpose(db[rows, :].astype(F32))
+        at_k = low + lax.broadcasted_iota(jnp.int32, (512, 256), 0)
+        at_q = row + lax.broadcasted_iota(jnp.int32, (512, 256), 1)
+        near = jnp.where(at_q >= at_k, nn(kb[low:width, :], q_t), -1e30)
+        top = jnp.max(near, axis=0, keepdims=True)
+        if j:
+            away = nn(kb[0:low, :], q_t)
+            top = jnp.maximum(top, jnp.max(away, axis=0, keepdims=True))
+        near = jnp.exp(near - top)
+        total = jnp.sum(near, axis=0, keepdims=True)
+        probs = near.astype(BF16)
+        if j:
+            away = jnp.exp(away - top)
+            total = total + jnp.sum(away, axis=0, keepdims=True)
+            probs = jnp.concatenate([away.astype(BF16), probs], axis=0)
+        scale = 1.0 / total
+        att_t = nn(vt_b[:, 0:width], probs) * scale
+        delta = jnp.sum(do_t * att_t, axis=0, keepdims=True) * scale
+        do_t = do_t * scale
+        high = delta.astype(BF16).astype(F32)
+        tail = lax.broadcasted_iota(jnp.int32, (8, 256), 0)
+        tail = jnp.where(tail == 0, -high, jnp.where(tail == 1, high - delta, 0.0))
+        right = jnp.concatenate([do_t, tail, jnp.zeros((56, 256), F32)], axis=0).astype(BF16)
+        d_s = (probs.astype(F32) * nn(vb[0:width, :], right)).astype(BF16)
+        blocks = pl.ds(8 * j + 4 * turn_off, 4)
+        blank = pl.ds(8 * j + 4 * (1 - turn_off), 4)
+        att_b[blocks] = jnp.transpose(att_t).reshape(4, 64, 64)
+        dq_b[blocks] = jnp.transpose(nn(kt_b[:, 0:width], d_s) * 0.125).reshape(4, 64, 64)
+        att_b[blank] = jnp.zeros((4, 64, 64), F32)
+        dq_b[blank] = jnp.zeros((4, 64, 64), F32)
+        d_k = nn(d_s, queries.astype(BF16)).reshape(8 * (j + 1), 64, 64)
+        d_v = nn(probs, jnp.transpose(do_t).astype(BF16)).reshape(8 * (j + 1), 64, 64)
+        if j == 3:
+            dk_b[...] = d_k
+            dv_b[...] = d_v
+        else:
+            dk_b[0 : 8 * (j + 1)] += d_k
+            dv_b[0 : 8 * (j + 1)] += d_v
+
+    tile(3)
+    for p in LATER:
+        reduce_step(p, 2)
+    for j in (2, 1, 0):
         tile(j)
-        if j > 0:
-            for p in LATER:
-                reduce_step(p, 3 - j)
     for i in range(32):
         t = table[i]
         zs[i] = jnp.concatenate([att_b[t], dq_b[t], dk_b[t], dv_b[t]], axis=1).astype(BF16)
@@ -462,17 +500,13 @@
         else:
             back[me] = ctotal[m]
     started += collect
+    for p in LATER:
+        reduce_step(p, 1)
     dh2_s[...] = nt(dup_s[...], wu[...])
     dh2 = dh2_s[...]
     gvec[2:3, 0:512] = jnp.sum(dh2 * xhat[...], axis=0, keepdims=True)
     gvec[3:4, 0:512] = jnp.sum(dh2, axis=0, keepdims=True)
     gvec[6:7, 0:512] = jnp.sum(dy.astype(F32), axis=0, keepdims=True)
-    for p in LATER:
-        value = reduce_end(p)
-        if p < 6:
-            asm2[:, LEFT[p] : LEFT[p] + COLS[p]] = value
-        else:
-            gdown_ref[:, LEFT[p] : LEFT[p] + COLS[p]] = value
     for copy in collect:
         copy.wait_recv()
 
@@ -500,18 +534,23 @@
     wide_loop(FIRST, 0, pack_from(ga))
     for p in FIRST:
         reduce_start(p)
+    for p in LATER:
+        reduce_step(p, 0)
     dh1 = nt(dqkv_s[...], wa[:, 0:1536])
     gvec[0:1, 0:512] = jnp.sum(dh1 * xhat[...], axis=0, keepdims=True)
     gvec[1:2, 0:512] = jnp.sum(dh1, axis=0, keepdims=True)
     gvec[4:5, 0:1024] = jnp.sum(dqkv_s[:, 0:1024].astype(F32), axis=0, keepdims=True)
     gvec[5:6, 0:512] = jnp.sum(dqkv_s[:, 1024:1536].astype(F32), axis=0, keepdims=True)
     spread_out = jnp.zeros((128, 128), F32)
+    left = 0
     for i, (n, off) in enumerate(SECTIONS_OUT):
-        pick, own = selectors(n, off)
-        value = jnp.where(own, gvec[i : i + 1, 0 : 128 * n], 0.0)
+        cols = slice(left, left + 128 * n)
+        left += 128 * n
+        value = gvec[i : i + 1, 0 : 128 * n]
         high = value.astype(BF16)
         low = (value - high.astype(F32)).astype(BF16)
-        spread_out = spread_out + nt(high, pick) + nt(low, pick)
+        pick, own = pick_out[:, cols], own_out[:, cols]
+        spread_out = spread_out + nt(own * high, pick) + nt(own * low, pick)
     gmat[...] = spread_out
     grads[SMALL][...] = jnp.zeros_like(grads[SMALL])
 
@@ -533,6 +572,12 @@
     ingrad_ref[0] = dy.astype(F32) + d_x * inv_s[:, 0:1]
     result = hid[0].astype(F32) + nn(mixed, wa[:, 1536:2048]) + mlp_s[...] + vecs[5:6, 0:512]
     out_ref[0] = result.astype(BF16)
+    for p in LATER:
+        value = reduce_end(p)
+        if p < 6:
+            asm2[:, LEFT[p] : LEFT[p] + COLS[p]] = value
+        else:
+            gdown_ref[:, LEFT[p] : LEFT[p] + COLS[p]] = value
     for k in (1, 0):
         for p in FIRST + (SMALL,):
             reduce_step(p, k)
@@ -572,12 +617,14 @@
     scratch += [VMEM((128, 128), F32)] * 2
     scratch += [VMEM((8, 2, 64, 256), BF16), VMEM((32, 64, 256), BF16), VMEM((32, 64, 256), BF16)]
     scratch += [VMEM((8, 2, 64, 256), BF16)] * 3
-    scratch += [VMEM((2048, 64), BF16)] * 4 + [VMEM((32, 64, 64), F32)] * 4
+    scratch += [VMEM((2048, 64), BF16)] * 2 + [VMEM((2048, 128), BF16), VMEM((2048, 64), BF16)]
+    scratch += [VMEM((32, 64, 64), F32)] * 4
     scratch += [VMEM((128, 512), F32)] + [VMEM((128, 128), F32)] * 3 + [VMEM((8, 2048), F32)] * 2
     scratch += [VMEM((128, 512), BF16)] * 2 + [VMEM((128, 2048), BF16)] * 2
     scratch += [VMEM((128, 512), F32)] * 2 + [VMEM((128, 1536), BF16)]
     scratch += [dma((3,))] * 4 + [dma((N, 9))] * 2 + [dma((N, 4))] * 2 + [dma((N, 10))] * 2
     scratch += [dma((7,)), dma((7,)), dma((8,)), dma((8,))] * 2
+    scratch += [VMEM((128, 6144), BF16)] * 4 + [VMEM((64, 2048), BF16)] * 2
     shape = jax.ShapeDtypeStruct
     return pl.pallas_call(
         block_kernel,

time: 111 us -> 108 us (0.973)
  Pallas kernels: 108 us -> 104 us
    pallas_call x1, Pallas kernels: 106 us -> 103 us  [run_block(): pl.pallas_call(block_kernel, out_shape=(shape((1, 128, 512), BF16), shape...]
where the time goes in v3:
time: 108 us
  Pallas kernels  104 us (96%)
  other arithmetic  1.28 us (1%)
    pallas_call x1, Pallas kernels, run_block(): pl.pallas_call(block_kernel, out_shape=(shape((1, 128, 512), BF16), shape...  103 us

profile of v3, /device:TPU:1, one launch (start us, length us, event | category | flops | bytes accessed | tf_op | source)
XLA Modules:
  0.0 107.6 jit_solution(12043077959246479816)
XLA Ops:
  0.6 0.0 copy-start.4
  0.7 0.0 copy-start.5
  0.7 0.0 copy-start.6
  0.7 0.0 copy-start.7
  0.7 0.0 copy-start.1
  0.7 0.0 copy-start.2
  0.7 0.0 copy-start.3
  0.7 0.6 copy-done.4
  1.3 0.0 copy-done.5
  1.3 0.0 copy-done.6
  1.3 0.0 copy-done.7
  1.4 0.0 copy-done.1
  1.4 0.0 copy-done.2
  1.4 0.0 copy-done.3
  1.4 0.1 concatenate.35
  1.5 0.0 copy-start
  1.5 0.6 pad_convert_fusion.small
  2.1 0.1 copy-done
  2.2 0.1 reshape.153
  2.3 0.1 reshape.154
  2.4 0.1 select_reduce_fusion
  2.4 0.6 pad_add_fusion.table
  3.0 102.5 %shard_map.263 = (bf16[1,128,512]{2,1,0:T(8,128)(2,1)}, f32[1,128,512]{2,1,0:T(8,128)}, f32[4,1536]{1,0:T(4,128)}, f32[4,512]{1,0:T(4,128)}, f32[4,2048]{1,0:T(4...) custom-call(s32[64]{0:T(128)} %pad_add_fusion.table, bf16[1,128,512]{2,1,0:T(8,128)(2,1)} %hid.1, ...), custom_call_target="tpu_custom_call" | custom-call | tf_op jit(solution)/shard_map/pallas_call | solution.py:629
  105.6 1.8 %shard_map.264 = (bf16[1,128,512]{2,1,0:T(8,128)(2,1)}, f32[1,128,512]{2,1,0:T(8,128)}, f32[4,1536]{1,0:T(4,128)}, f32[4,512]{1,0:T(4,128)}, f32[4,2048]{1,0:T(4...) custom-call(bf16[1,128,512]{2,1,0:T(8,128)(2,1)} %get-tuple-element., ...), custom_call_target="tpu_custom_call" | custom-call | tf_op jit(solution)/shard_map/pallas_call | solution.py:654
  (1 shorter events, 0.0 us)
Async XLA Ops:
  0.6 0.7 copy-start.4
  0.7 0.7 copy-start.5
  0.7 0.7 copy-start.6
  0.7 0.7 copy-start.7
  0.7 0.7 copy-start.1
  0.7 0.7 copy-start.2
  0.7 0.7 copy-start.3
  1.5 0.7 copy-start

commit v4 on v3

--- a/solution.py
+++ b/solution.py
@@ -139,6 +139,18 @@
     for p in (6, 7):
         bufs[p][core, slots[p]] = w_lower[:, LEFT[p] : LEFT[p] + COLS[p]]
     bufs[SMALL][core, slots[SMALL]] = small[...]
+    x = hid[0].astype(F32)
+    center = x - jnp.mean(x, axis=1, keepdims=True)
+    inv = lax.rsqrt(jnp.mean(center * center, axis=1, keepdims=True) + EPS)
+    xhat[...] = center * inv
+    inv_s[...] = jnp.broadcast_to(inv, (128, 128))
+    places = jnp.transpose(jnp.broadcast_to(pos[...].astype(F32), (128, 128)))
+    angle = places * freq[...]
+    lane = lax.broadcasted_iota(jnp.int32, (128, 128), 1)
+    lane = lane - 64 * (lane >= 64).astype(jnp.int32)
+    sine = jnp.sin(angle)
+    cos_s[...] = jnp.cos(angle)
+    sin_s[...] = jnp.where(lane < 8, -sine, sine)
     pl.semaphore_wait(barrier, len(everyone))
 
     quad = []
@@ -194,21 +206,7 @@
         bufs[p][core, slots[p]] = asm[:, LEFT[p] : LEFT[p] + COLS[p]].astype(BF16)
         gather_send(p, 0)
 
-    x = hid[0].astype(F32)
-    center = x - jnp.mean(x, axis=1, keepdims=True)
-    inv = lax.rsqrt(jnp.mean(center * center, axis=1, keepdims=True) + EPS)
-    xhat[...] = center * inv
-    inv_s[...] = jnp.broadcast_to(inv, (128, 128))
-    places = jnp.transpose(jnp.broadcast_to(pos[...].astype(F32), (128, 128)))
-    angle = places * freq[...]
-    lane = lax.broadcasted_iota(jnp.int32, (128, 128), 1)
-    lane = lane - 64 * (lane >= 64).astype(jnp.int32)
-    sine = jnp.sin(angle)
-    cos_s[...] = jnp.cos(angle)
-    sin_s[...] = jnp.where(lane < 8, -sine, sine)
-    for sections, picks, owns in (
-        (SECTIONS_IN, pick_in, own_in), (SECTIONS_OUT, pick_out, own_out)
-    ):
+    def build(sections, picks, owns):
         left = 0
         for n, off in sections:
             pick, own = selectors(n, off)
@@ -216,9 +214,11 @@
             owns[:, left : left + 128 * n] = own
             left += 128 * n
 
+    build(SECTIONS_IN, pick_in, own_in)
     for p in (SMALL,) + FIRST + LATER:
         gather_wait(p, 0)
         gather_send(p, 1)
+    build(SECTIONS_OUT, pick_out, own_out)
     for p in (SMALL,) + FIRST:
         gather_wait(p, 1)
         gather_send(p, 2)
@@ -376,10 +376,13 @@
                 adds[p, k + 1, d].wait_recv()
             base, total = block(p, k + 1)
             others = [offset(k + 1) + d * total for d in range(3)]
-        unit = min(total, 4)
+        unit = min(total, 8 if len(others) == 1 else 4)
 
         def body(i, carry):
             here = pl.ds(base + i * unit, unit)
+            if len(others) == 1:
+                grads[p][core, here] += recv[p][pl.ds(others[0] + i * unit, unit)]
+                return carry
             value = grads[p][core, here].astype(F32)
             for other in others:
                 value = value + recv[p][pl.ds(other + i * unit, unit)].astype(F32)
@@ -449,8 +452,8 @@
             probs = jnp.concatenate([away.astype(BF16), probs], axis=0)
         scale = 1.0 / total
         att_t = nn(vt_b[:, 0:width], probs) * scale
-        delta = jnp.sum(do_t * att_t, axis=0, keepdims=True) * scale
-        do_t = do_t * scale
+        do_t = (do_t * scale).astype(BF16).astype(F32)
+        delta = jnp.sum(do_t * att_t, axis=0, keepdims=True)
         high = delta.astype(BF16).astype(F32)
         tail = lax.broadcasted_iota(jnp.int32, (8, 256), 0)
         tail = jnp.where(tail == 0, -high, jnp.where(tail == 1, high - delta, 0.0))
@@ -534,13 +537,13 @@
     wide_loop(FIRST, 0, pack_from(ga))
     for p in FIRST:
         reduce_start(p)
-    for p in LATER:
-        reduce_step(p, 0)
     dh1 = nt(dqkv_s[...], wa[:, 0:1536])
     gvec[0:1, 0:512] = jnp.sum(dh1 * xhat[...], axis=0, keepdims=True)
     gvec[1:2, 0:512] = jnp.sum(dh1, axis=0, keepdims=True)
     gvec[4:5, 0:1024] = jnp.sum(dqkv_s[:, 0:1024].astype(F32), axis=0, keepdims=True)
     gvec[5:6, 0:512] = jnp.sum(dqkv_s[:, 1024:1536].astype(F32), axis=0, keepdims=True)
+    for p in FIRST:
+        reduce_step(p, 2)
     spread_out = jnp.zeros((128, 128), F32)
     left = 0
     for i, (n, off) in enumerate(SECTIONS_OUT):
@@ -562,25 +565,26 @@
 
     lax.fori_loop(0, 32, small_grads, 0)
     reduce_start(SMALL)
-    for p in FIRST:
-        reduce_step(p, 2)
+    result = hid[0].astype(F32) + nn(mixed, wa[:, 1536:2048]) + mlp_s[...] + vecs[5:6, 0:512]
+    out_ref[0] = result.astype(BF16)
     reduce_step(SMALL, 2)
     d_norm = dh1 * vecs[0:1, 0:512] + dh2_s[...] * vecs[2:3, 0:512]
     normed = xhat[...]
     d_x = d_norm - jnp.mean(d_norm, axis=1, keepdims=True)
     d_x = d_x - normed * jnp.mean(d_norm * normed, axis=1, keepdims=True)
     ingrad_ref[0] = dy.astype(F32) + d_x * inv_s[:, 0:1]
-    result = hid[0].astype(F32) + nn(mixed, wa[:, 1536:2048]) + mlp_s[...] + vecs[5:6, 0:512]
-    out_ref[0] = result.astype(BF16)
+    for p in LATER:
+        reduce_step(p, 0)
+    for p in FIRST + (SMALL,):
+        reduce_step(p, 1)
     for p in LATER:
         value = reduce_end(p)
         if p < 6:
             asm2[:, LEFT[p] : LEFT[p] + COLS[p]] = value
         else:
             gdown_ref[:, LEFT[p] : LEFT[p] + COLS[p]] = value
-    for k in (1, 0):
-        for p in FIRST + (SMALL,):
-            reduce_step(p, k)
+    for p in FIRST + (SMALL,):
+        reduce_step(p, 0)
     for p in FIRST:
         asm2[:, LEFT[p] : LEFT[p] + COLS[p]] = reduce_end(p)
     gsmall_ref[...] = reduce_end(SMALL)

time: 108 us -> 106 us (0.981)
    pallas_call x1, Pallas kernels: 103 us -> 101 us  [run_block(): pl.pallas_call(block_kernel, out_shape=(shape((1, 128, 512), BF16), shape...]
where the time goes in v4:
time: 106 us
  Pallas kernels  103 us (97%)
  other arithmetic  1.28 us (1%)
    pallas_call x1, Pallas kernels, run_block(): pl.pallas_call(block_kernel, out_shape=(shape((1, 128, 512), BF16), shape...  101 us

profile of v4, /device:TPU:1, one launch (start us, length us, event | category | flops | bytes accessed | tf_op | source)
XLA Modules:
  0.0 106.2 jit_solution(17527031519786411994)
XLA Ops:
  0.6 0.0 copy-start.4
  0.7 0.0 copy-start.5
  0.7 0.0 copy-start.6
  0.7 0.0 copy-start.7
  0.7 0.0 copy-start.1
  0.7 0.0 copy-start.2
  0.7 0.0 copy-start.3
  0.7 0.6 copy-done.4
  1.3 0.0 copy-done.5
  1.3 0.0 copy-done.6
  1.3 0.0 copy-done.7
  1.4 0.0 copy-done.1
  1.4 0.0 copy-done.2
  1.4 0.0 copy-done.3
  1.4 0.1 concatenate.35
  1.5 0.0 copy-start
  1.5 0.6 pad_convert_fusion.small
  2.1 0.1 copy-done
  2.2 0.1 reshape.153
  2.3 0.1 reshape.154
  2.4 0.1 select_reduce_fusion
  2.4 0.6 pad_add_fusion.table
  3.0 101.1 %shard_map.263 = (bf16[1,128,512]{2,1,0:T(8,128)(2,1)}, f32[1,128,512]{2,1,0:T(8,128)}, f32[4,1536]{1,0:T(4,128)}, f32[4,512]{1,0:T(4,128)}, f32[4,2048]{1,0:T(4...) custom-call(s32[64]{0:T(128)} %pad_add_fusion.table, bf16[1,128,512]{2,1,0:T(8,128)(2,1)} %hid.1, ...), custom_call_target="tpu_custom_call" | custom-call | tf_op jit(solution)/shard_map/pallas_call | solution.py:633
  104.2 1.8 %shard_map.264 = (bf16[1,128,512]{2,1,0:T(8,128)(2,1)}, f32[1,128,512]{2,1,0:T(8,128)}, f32[4,1536]{1,0:T(4,128)}, f32[4,512]{1,0:T(4,128)}, f32[4,2048]{1,0:T(4...) custom-call(bf16[1,128,512]{2,1,0:T(8,128)(2,1)} %get-tuple-element., ...), custom_call_target="tpu_custom_call" | custom-call | tf_op jit(solution)/shard_map/pallas_call | solution.py:658
  (1 shorter events, 0.0 us)
Async XLA Ops:
  0.6 0.7 copy-start.4
  0.7 0.7 copy-start.5
  0.7 0.7 copy-start.6
  0.7 0.7 copy-start.7
  0.7 0.7 copy-start.1
  0.7 0.7 copy-start.2
  0.7 0.7 copy-start.3
  1.5 0.7 copy-start

commit v5 on v4

--- a/solution.py
+++ b/solution.py
@@ -14,12 +14,16 @@
 LIMIT = 60 * 1024 * 1024
 
 ORDERS = ((0, 1, 2), (1, 2, 0), (2, 0, 1))
-ORDER_OF = (0, 1, 2, 1, 0, 1, 1, 2)
-COLS = (256, 128, 128, 128, 256, 256, 128, 384)
-LEFT = (0, 256, 384, 0, 512, 768, 0, 128)
-N = 8
-FIRST, SMALL, LATER = (0, 1, 2), 3, (4, 5, 6, 7)
-TILES = [((8, 128), F32) if p == SMALL else ((16, COLS[p]), BF16) for p in range(N)]
+ORDER_OF = (0, 1, 2, 1, 0, 1, 2)
+N = 7
+FIRST, SMALL, LATER = (0, 1, 2), 3, (4, 5, 6)
+TILES = [((16, c), BF16) for c in (256, 128, 128, 0, 384, 256, 384)]
+TILES[SMALL] = ((8, 128), F32)
+GATHERED = list(TILES)
+GATHERED[1] = ((16, 256), BF16)
+FIRST_PIECES = ((0, 0, 256, 0), (1, 0, 128, 256), (2, 0, 128, 384))
+UP_PIECES = ((4, 0, 384, 0), (5, 0, 128, 384))
+DOWN_PIECES = ((5, 128, 128, 0), (6, 0, 384, 128))
 SECTIONS_IN = ((4, 0), (4, 4), (4, 8), (4, 12), (12, 16), (4, 28), (16, 32))
 SECTIONS_OUT = ((4, 0), (4, 4), (4, 8), (4, 12), (8, 16), (4, 24), (4, 28), (16, 32))
 
@@ -128,6 +132,10 @@
     slots = [slot_of(p, at) for p in range(N)]
     started = []
 
+    def settle():
+        while started:
+            started.pop(0).wait_send()
+
     squad[...] = jnp.zeros_like(squad)
     qkv_rows = w_qkv[...].astype(F32)
     up_rows = w_upper[...].astype(F32)
@@ -136,9 +144,9 @@
     squad[3, 0:4, 0:512] = w_proj[...].astype(F32)
     for t in range(4):
         squad[t, 0:4, 512:1024] = up_rows[:, 512 * t : 512 * (t + 1)]
-    for p in (6, 7):
-        bufs[p][core, slots[p]] = w_lower[:, LEFT[p] : LEFT[p] + COLS[p]]
-    bufs[SMALL][core, slots[SMALL]] = small[...]
+    for p, left, cols, there in DOWN_PIECES:
+        bufs[p][core, slots[p], :, left : left + cols] = w_lower[:, there : there + cols]
+    bufs[1][core, slots[1], :, 128:256] = small[...]
     x = hid[0].astype(F32)
     center = x - jnp.mean(x, axis=1, keepdims=True)
     inv = lax.rsqrt(jnp.mean(center * center, axis=1, keepdims=True) + EPS)
@@ -175,35 +183,28 @@
                 part, part, ags.at[p, 3 * k + d], agr.at[p, 3 * k + d], axis_peers[axis][d]
             )
             started.append(hops[p, k, d])
-        if k == 2:
-            fwd[p, 3] = send(part, part, fws.at[p, 3], fwr.at[p, 3], sibling)
-            started.append(fwd[p, 3])
 
     def gather_wait(p, k):
         for d in range(3):
             hops[p, k, d].wait_recv()
 
     def gather_forward(p):
-        axis = ORDERS[ORDER_OF[p]][2]
-        for d in range(3):
-            hops[p, 2, d].wait_recv()
-            base = lax.rem(at[axis] + 3 - d, 4) * 16
-            part = bufs[p].at[core, pl.ds(base, 16)]
-            fwd[p, d] = send(part, part, fws.at[p, d], fwr.at[p, d], sibling)
-            started.append(fwd[p, d])
+        gather_wait(p, 2)
+        plane = bufs[p].at[core]
+        fwd[p] = send(plane, plane, fws.at[p], fwr.at[p], sibling)
+        started.append(fwd[p])
 
     def gather_done(p):
-        for d in range(4):
-            fwd[p, d].wait_recv()
-
-    for p in (SMALL, 6, 7):
-        gather_send(p, 0)
+        fwd[p].wait_recv()
+
+    gather_send(6, 0)
     for copy in quad:
         copy.wait_recv()
     for t in range(4):
         asm[4 * t : 4 * t + 4, :] = rquad[t, 0:4, :]
-    for p in (0, 1, 2, 4, 5):
-        bufs[p][core, slots[p]] = asm[:, LEFT[p] : LEFT[p] + COLS[p]].astype(BF16)
+    for p, left, cols, there in FIRST_PIECES + UP_PIECES:
+        there = there if p < 3 else there + 512
+        bufs[p][core, slots[p], :, left : left + cols] = asm[:, there : there + cols].astype(BF16)
         gather_send(p, 0)
 
     def build(sections, picks, owns):
@@ -215,14 +216,14 @@
             left += 128 * n
 
     build(SECTIONS_IN, pick_in, own_in)
-    for p in (SMALL,) + FIRST + LATER:
+    for p in FIRST + LATER:
         gather_wait(p, 0)
         gather_send(p, 1)
     build(SECTIONS_OUT, pick_out, own_out)
-    for p in (SMALL,) + FIRST:
+    for p in FIRST:
         gather_wait(p, 1)
         gather_send(p, 2)
-    for p in (SMALL,) + FIRST:
+    for p in FIRST:
         gather_forward(p)
     for p in LATER:
         gather_wait(p, 1)
@@ -232,14 +233,13 @@
         x_lo = lax.rem(lax.div(row, 4), 2)
         return [(t // 2) * 2 + x_lo, lax.rem(row, 4), lax.div(row, 8)], t % 2
 
-    def wide_loop(streams, left0, store):
+    def wide_loop(pieces, store):
         def body(row, carry):
             rows = pl.ds(pl.multiple_of(row * 16, 16), 16)
             for t in range(4):
                 where, c = place_of(row, t)
-                for p in streams:
-                    left = 512 * t + LEFT[p] - left0
-                    store(p, c, slot_of(p, where), rows, left)
+                for p, left, cols, there in pieces:
+                    store(p, c, slot_of(p, where), rows, left, cols, 512 * t + there)
             return carry
 
         lax.fori_loop(0, 32, body, 0)
@@ -249,30 +249,30 @@
             for t in range(4):
                 where, c = place_of(row, t)
                 rows = pl.ds(pl.multiple_of(row * 64 + t * 16, 16), 16)
-                for p in (6, 7):
-                    store(p, c, slot_of(p, where), rows, LEFT[p])
+                for p, left, cols, there in DOWN_PIECES:
+                    store(p, c, slot_of(p, where), rows, left, cols, there)
             return carry
 
         lax.fori_loop(0, 32, body, 0)
 
     def unpack_to(dst):
-        def store(p, c, slot, rows, left):
-            dst[rows, left : left + COLS[p]] = bufs[p][c, slot]
+        def store(p, c, slot, rows, left, cols, there):
+            dst[rows, there : there + cols] = bufs[p][c, slot, :, left : left + cols]
 
         return store
 
     def pack_from(src):
-        def store(p, c, slot, rows, left):
-            grads[p][c, slot] = src[rows, left : left + COLS[p]]
+        def store(p, c, slot, rows, left, cols, there):
+            grads[p][c, slot, :, left : left + cols] = src[rows, there : there + cols]
 
         return store
 
-    gather_done(SMALL)
+    gather_done(1)
 
     def small_rows(row, carry):
         for t in range(4):
             where, c = place_of(row, t)
-            smat[pl.ds(row * 4 + t, 1), :] = bufs[SMALL][c, slot_of(SMALL, where), 0:1, :]
+            smat[pl.ds(row * 4 + t, 1), :] = bufs[1][c, slot_of(1, where), :, 128:256].astype(F32)[0:1]
         return carry
 
     lax.fori_loop(0, 32, small_rows, 0)
@@ -287,9 +287,9 @@
     normed = xhat[...]
     h1_s[...] = (normed * vecs[0:1, 0:512] + vecs[1:2, 0:512]).astype(BF16)
     h2_s[...] = (normed * vecs[2:3, 0:512] + vecs[3:4, 0:512]).astype(BF16)
-    for p in FIRST:
+    for p in (0, 2):
         gather_done(p)
-    wide_loop(FIRST, 0, unpack_to(wa))
+    wide_loop(FIRST_PIECES, unpack_to(wa))
 
     dy = dy_ref[0]
     parts = [nn(h1_s[...], wa[:, 512 * i : 512 * (i + 1)]) for i in range(3)]
@@ -329,7 +329,7 @@
         gather_forward(p)
     for p in LATER:
         gather_done(p)
-    wide_loop((4, 5), 512, unpack_to(wu))
+    wide_loop(UP_PIECES, unpack_to(wu))
     tall_loop(unpack_to(wd))
 
     def mlp(t):
@@ -410,7 +410,7 @@
             value = value + recv[p][offset(0) + d].astype(F32)
         return value
 
-    wide_loop((4, 5), 512, pack_from(gu))
+    wide_loop(UP_PIECES, pack_from(gu))
     tall_loop(pack_from(gd))
     for p in LATER:
         reduce_start(p)
@@ -510,6 +510,7 @@
     gvec[2:3, 0:512] = jnp.sum(dh2 * xhat[...], axis=0, keepdims=True)
     gvec[3:4, 0:512] = jnp.sum(dh2, axis=0, keepdims=True)
     gvec[6:7, 0:512] = jnp.sum(dy.astype(F32), axis=0, keepdims=True)
+    settle()
     for copy in collect:
         copy.wait_recv()
 
@@ -534,7 +535,7 @@
         ga[:, 512 * t : 512 * (t + 1)] = tn(
             h1_s[...], dqkv_s[:, 512 * t : 512 * (t + 1)]
         ).astype(BF16)
-    wide_loop(FIRST, 0, pack_from(ga))
+    wide_loop(FIRST_PIECES, pack_from(ga))
     for p in FIRST:
         reduce_start(p)
     dh1 = nt(dqkv_s[...], wa[:, 0:1536])
@@ -579,14 +580,16 @@
         reduce_step(p, 1)
     for p in LATER:
         value = reduce_end(p)
-        if p < 6:
-            asm2[:, LEFT[p] : LEFT[p] + COLS[p]] = value
-        else:
-            gdown_ref[:, LEFT[p] : LEFT[p] + COLS[p]] = value
+        for p_of, left, cols, there in UP_PIECES:
+            if p_of == p:
+                asm2[:, 512 + there : 512 + there + cols] = value[:, left : left + cols]
+        for p_of, left, cols, there in DOWN_PIECES:
+            if p_of == p:
+                gdown_ref[:, there : there + cols] = value[:, left : left + cols]
     for p in FIRST + (SMALL,):
         reduce_step(p, 0)
-    for p in FIRST:
-        asm2[:, LEFT[p] : LEFT[p] + COLS[p]] = reduce_end(p)
+    for p, _, cols, there in FIRST_PIECES:
+        asm2[:, there : there + cols] = reduce_end(p)
     gsmall_ref[...] = reduce_end(SMALL)
     squad2[...] = jnp.zeros_like(squad2)
     for t in range(4):
@@ -599,8 +602,8 @@
                 peer,
             )
         )
-    started += quad
     rquad2[q] = squad2[q]
+    settle()
     for copy in quad:
         copy.wait_recv()
     for t in range(3):
@@ -608,13 +611,14 @@
     gproj_ref[...] = rquad2[3, 0:4, 0:512]
     for t in range(4):
         gup_ref[:, 512 * t : 512 * (t + 1)] = rquad2[t, 0:4, 512:1024]
-    for copy in started:
+    for copy in quad:
         copy.wait_send()
 
 
 def run_block(*args):
     dma = pltpu.SemaphoreType.DMA
-    scratch = [VMEM((2, 64) + tile, dtype) for tile, dtype in TILES] * 2
+    scratch = [VMEM((2, 64) + tile, dtype) for tile, dtype in GATHERED]
+    scratch += [VMEM((2, 64) + tile, dtype) for tile, dtype in TILES]
     scratch += [VMEM((128,) + tile, dtype) for tile, dtype in TILES]
     scratch += [VMEM((4, 8, 1024), F32)] * 4 + [VMEM((16, 1024), F32)] * 2
     scratch += [VMEM((512, 2048), BF16), VMEM((512, 2048), BF16), VMEM((2048, 512), BF16)] * 2
@@ -626,7 +630,7 @@
     scratch += [VMEM((128, 512), F32)] + [VMEM((128, 128), F32)] * 3 + [VMEM((8, 2048), F32)] * 2
     scratch += [VMEM((128, 512), BF16)] * 2 + [VMEM((128, 2048), BF16)] * 2
     scratch += [VMEM((128, 512), F32)] * 2 + [VMEM((128, 1536), BF16)]
-    scratch += [dma((3,))] * 4 + [dma((N, 9))] * 2 + [dma((N, 4))] * 2 + [dma((N, 10))] * 2
+    scratch += [dma((3,))] * 4 + [dma((N, 9))] * 2 + [dma((N,))] * 2 + [dma((N, 10))] * 2
     scratch += [dma((7,)), dma((7,)), dma((8,)), dma((8,))] * 2
     scratch += [VMEM((128, 6144), BF16)] * 4 + [VMEM((64, 2048), BF16)] * 2
     shape = jax.ShapeDtypeStruct
@@ -670,8 +674,8 @@
 ):
     small = jnp.concatenate(
         [norm1_gain, norm1_bias, norm2_gain, norm2_bias, qkv_bias, out_bias, up_bias]
-    ).astype(F32)
-    small = jnp.pad(small[None], ((0, 7), (0, 80)))
+    )
+    small = jnp.pad(small[None], ((0, 15), (0, 80)))
     held = block_order.reshape(8, 2, 2).transpose(1, 0, 2).reshape(32)
     ids = jnp.arange(32, dtype=jnp.int32)
     inverse = jnp.sum(jnp.where(held[:, None] == ids[None, :], ids[:, None], 0), axis=0)

time: 106 us -> 108 us (1.019)
  local copies, waits for them, and re-layouts: 1.03 us -> 5.6 us
  Pallas kernels: 103 us -> 101 us
    concatenate x1, local copies, waits for them, and re-layouts: 0.1 us -> 4.77 us  [per_device(): jnp.concatenate([norm1_gain, norm1_bias, norm2_gain, norm2_bias, qkv_bias...]
    pallas_call x1, Pallas kernels: 101 us -> 98.9 us  [run_block(): pl.pallas_call(block_kernel, out_shape=(shape((1, 128, 512), BF16), shape...]
where the time goes in v5:
time: 108 us
  Pallas kernels  101 us (94%)
  local copies, waits for them, and re-layouts  5.6 us (5%)
    pallas_call x1, Pallas kernels, run_block(): pl.pallas_call(block_kernel, out_shape=(shape((1, 128, 512), BF16), shape...  98.9 us
    concatenate x1, local copies, waits for them, and re-layouts, per_device(): jnp.concatenate([norm1_gain, norm1_bias, norm2_gain, norm2_bias, qkv_bias...  4.77 us

profile of v5, /device:TPU:1, one launch (start us, length us, event | category | flops | bytes accessed | tf_op | source)
XLA Modules:
  0.0 107.8 jit_solution(12617949572190067190)
XLA Ops:
  0.6 4.8 %concatenate.7 = bf16[48]{0:T(256)(128)(2,1)S(1)} concatenate(bf16[4]{0:T(256)(128)(2,1)} %param.19, bf16[4]{0:T(256)(128)(2,1)} %param.20, bf16[4]{0:T(256)(128)(2,1)} %param.21, bf16[4]{0:T(256)(128)(2,1)} %param.22, bf16[12]{0:T(256)(128)(2,1)} %param.24, bf16[4]{0:T(256)(128)(2,1)} %param.26, bf16[16]{0:T(256)(128)(2,1)} %param.28), dimensions={0} | concatenate | bytes 192 | tf_op jit(solution)/shard_map/concatenate | solution.py:675
  5.4 0.0 copy-start
  5.4 0.6 pad.4.small
  6.0 0.1 copy-done
  6.1 0.1 reshape.59
  6.2 0.1 reshape.60
  6.3 0.1 select_reduce_fusion
  6.4 0.6 pad_add_fusion.table
  7.0 98.9 %shard_map.263 = (bf16[1,128,512]{2,1,0:T(8,128)(2,1)}, f32[1,128,512]{2,1,0:T(8,128)}, f32[4,1536]{1,0:T(4,128)}, f32[4,512]{1,0:T(4,128)}, f32[4,2048]{1,0:T(4...) custom-call(s32[64]{0:T(128)} %pad_add_fusion.table, bf16[1,128,512]{2,1,0:T(8,128)(2,1)} %hid.1, ...), custom_call_target="tpu_custom_call" | custom-call | tf_op jit(solution)/shard_map/pallas_call | solution.py:637
  105.8 1.8 %shard_map.264 = (bf16[1,128,512]{2,1,0:T(8,128)(2,1)}, f32[1,128,512]{2,1,0:T(8,128)}, f32[4,1536]{1,0:T(4,128)}, f32[4,512]{1,0:T(4,128)}, f32[4,2048]{1,0:T(4...) custom-call(bf16[1,128,512]{2,1,0:T(8,128)(2,1)} %get-tuple-element., ...), custom_call_target="tpu_custom_call" | custom-call | tf_op jit(solution)/shard_map/pallas_call | solution.py:662
  (1 shorter events, 0.0 us)
Async XLA Ops:
  5.4 0.7 copy-start

commit v6 on v5

--- a/solution.py
+++ b/solution.py
@@ -229,31 +229,30 @@
         gather_wait(p, 1)
         gather_send(p, 2)
 
-    def place_of(row, t):
-        x_lo = lax.rem(lax.div(row, 4), 2)
-        return [(t // 2) * 2 + x_lo, lax.rem(row, 4), lax.div(row, 8)], t % 2
+    def each_device(step):
+        def body(z, carry):
+            for low in range(8):
+                for t in range(4):
+                    step(z, low, t, [(t // 2) * 2 + low // 4, low % 4, z], t % 2)
+            return carry
+
+        lax.fori_loop(0, 4, body, 0)
 
     def wide_loop(pieces, store):
-        def body(row, carry):
-            rows = pl.ds(pl.multiple_of(row * 16, 16), 16)
-            for t in range(4):
-                where, c = place_of(row, t)
-                for p, left, cols, there in pieces:
-                    store(p, c, slot_of(p, where), rows, left, cols, 512 * t + there)
-            return carry
-
-        lax.fori_loop(0, 32, body, 0)
+        def step(z, low, t, where, c):
+            rows = pl.ds(pl.multiple_of(z * 128 + low * 16, 16), 16)
+            for p, left, cols, there in pieces:
+                store(p, c, slot_of(p, where), rows, left, cols, 512 * t + there)
+
+        each_device(step)
 
     def tall_loop(store):
-        def body(row, carry):
-            for t in range(4):
-                where, c = place_of(row, t)
-                rows = pl.ds(pl.multiple_of(row * 64 + t * 16, 16), 16)
-                for p, left, cols, there in DOWN_PIECES:
-                    store(p, c, slot_of(p, where), rows, left, cols, there)
-            return carry
-
-        lax.fori_loop(0, 32, body, 0)
+        def step(z, low, t, where, c):
+            rows = pl.ds(pl.multiple_of(z * 512 + low * 64 + t * 16, 16), 16)
+            for p, left, cols, there in DOWN_PIECES:
+                store(p, c, slot_of(p, where), rows, left, cols, there)
+
+        each_device(step)
 
     def unpack_to(dst):
         def store(p, c, slot, rows, left, cols, there):
@@ -269,13 +268,11 @@
 
     gather_done(1)
 
-    def small_rows(row, carry):
-        for t in range(4):
-            where, c = place_of(row, t)
-            smat[pl.ds(row * 4 + t, 1), :] = bufs[1][c, slot_of(1, where), :, 128:256].astype(F32)[0:1]
-        return carry
-
-    lax.fori_loop(0, 32, small_rows, 0)
+    def small_rows(z, low, t, where, c):
+        tile = bufs[1][c, slot_of(1, where), :, 128:256].astype(F32)
+        smat[pl.ds(z * 32 + (low * 4 + t), 1), :] = tile[0:1]
+
+    each_device(small_rows)
     tiles = smat[...].astype(BF16)
     left = 0
     for i, (n, off) in enumerate(SECTIONS_IN):
@@ -558,13 +555,11 @@
     gmat[...] = spread_out
     grads[SMALL][...] = jnp.zeros_like(grads[SMALL])
 
-    def small_grads(row, carry):
-        for t in range(4):
-            where, c = place_of(row, t)
-            grads[SMALL][c, slot_of(SMALL, where), 0:1, :] = gmat[pl.ds(row * 4 + t, 1), :]
-        return carry
-
-    lax.fori_loop(0, 32, small_grads, 0)
+    def small_grads(z, low, t, where, c):
+        row = gmat[pl.ds(z * 32 + (low * 4 + t), 1), :]
+        grads[SMALL][c, slot_of(SMALL, where), 0:1, :] = row
+
+    each_device(small_grads)
     reduce_start(SMALL)
     result = hid[0].astype(F32) + nn(mixed, wa[:, 1536:2048]) + mlp_s[...] + vecs[5:6, 0:512]
     out_ref[0] = result.astype(BF16)

time: 108 us -> 106 us (0.981)
  Pallas kernels: 101 us -> 98.8 us
    pallas_call x1, Pallas kernels: 98.9 us -> 97 us  [run_block(): pl.pallas_call(block_kernel, out_shape=(shape((1, 128, 512), BF16), shape...]
where the time goes in v6:
time: 106 us
  Pallas kernels  98.8 us (93%)
  local copies, waits for them, and re-layouts  5.6 us (5%)
    pallas_call x1, Pallas kernels, run_block(): pl.pallas_call(block_kernel, out_shape=(shape((1, 128, 512), BF16), shape...  97 us
    concatenate x1, local copies, waits for them, and re-layouts, per_device(): jnp.concatenate([norm1_gain, norm1_bias, norm2_gain, norm2_bias, qkv_bias...  4.77 us

profile of v6, /device:TPU:1, one launch (start us, length us, event | category | flops | bytes accessed | tf_op | source)
XLA Modules:
  0.0 106.0 jit_solution(13191915327758774163)
XLA Ops:
  0.6 4.8 %concatenate.7 = bf16[48]{0:T(256)(128)(2,1)S(1)} concatenate(bf16[4]{0:T(256)(128)(2,1)} %param.19, bf16[4]{0:T(256)(128)(2,1)} %param.20, bf16[4]{0:T(256)(128)(2,1)} %param.21, bf16[4]{0:T(256)(128)(2,1)} %param.22, bf16[12]{0:T(256)(128)(2,1)} %param.24, bf16[4]{0:T(256)(128)(2,1)} %param.26, bf16[16]{0:T(256)(128)(2,1)} %param.28), dimensions={0} | concatenate | bytes 192 | tf_op jit(solution)/shard_map/concatenate | solution.py:670
  5.4 0.0 copy-start
  5.4 0.6 pad.4.small
  6.0 0.1 copy-done
  6.1 0.1 reshape.59
  6.2 0.1 reshape.60
  6.3 0.1 select_reduce_fusion
  6.4 0.6 pad_add_fusion.table
  7.0 97.0 %shard_map.263 = (bf16[1,128,512]{2,1,0:T(8,128)(2,1)}, f32[1,128,512]{2,1,0:T(8,128)}, f32[4,1536]{1,0:T(4,128)}, f32[4,512]{1,0:T(4,128)}, f32[4,2048]{1,0:T(4...) custom-call(s32[64]{0:T(128)} %pad_add_fusion.table, bf16[1,128,512]{2,1,0:T(8,128)(2,1)} %hid.1, ...), custom_call_target="tpu_custom_call" | custom-call | tf_op jit(solution)/shard_map/pallas_call | solution.py:632
  104.0 1.8 %shard_map.264 = (bf16[1,128,512]{2,1,0:T(8,128)(2,1)}, f32[1,128,512]{2,1,0:T(8,128)}, f32[4,1536]{1,0:T(4,128)}, f32[4,512]{1,0:T(4,128)}, f32[4,2048]{1,0:T(4...) custom-call(bf16[1,128,512]{2,1,0:T(8,128)(2,1)} %get-tuple-element., ...), custom_call_target="tpu_custom_call" | custom-call | tf_op jit(solution)/shard_map/pallas_call | solution.py:657
  (1 shorter events, 0.0 us)
Async XLA Ops:
  5.4 0.7 copy-start

commit v7 on v6

--- a/solution.py
+++ b/solution.py
@@ -274,16 +274,19 @@
 
     each_device(small_rows)
     tiles = smat[...].astype(BF16)
-    left = 0
-    for i, (n, off) in enumerate(SECTIONS_IN):
-        cols = slice(left, left + 128 * n)
-        left += 128 * n
-        vecs[i : i + 1, 0 : 128 * n] = jnp.sum(
-            own_in[:, cols].astype(F32) * nn(tiles, pick_in[:, cols]), axis=0, keepdims=True
-        )
+
+    def vectors(wanted):
+        for i in wanted:
+            n = SECTIONS_IN[i][0]
+            left = 128 * sum(m for m, _ in SECTIONS_IN[:i])
+            cols = slice(left, left + 128 * n)
+            vecs[i : i + 1, 0 : 128 * n] = jnp.sum(
+                own_in[:, cols].astype(F32) * nn(tiles, pick_in[:, cols]), axis=0, keepdims=True
+            )
+
+    vectors((0, 1, 4))
     normed = xhat[...]
     h1_s[...] = (normed * vecs[0:1, 0:512] + vecs[1:2, 0:512]).astype(BF16)
-    h2_s[...] = (normed * vecs[2:3, 0:512] + vecs[3:4, 0:512]).astype(BF16)
     for p in (0, 2):
         gather_done(p)
     wide_loop(FIRST_PIECES, unpack_to(wa))
@@ -324,6 +327,8 @@
 
     for p in LATER:
         gather_forward(p)
+    vectors((2, 3, 5, 6))
+    h2_s[...] = (xhat[...] * vecs[2:3, 0:512] + vecs[3:4, 0:512]).astype(BF16)
     for p in LATER:
         gather_done(p)
     wide_loop(UP_PIECES, unpack_to(wu))
@@ -499,6 +504,7 @@
             )
         else:
             back[me] = ctotal[m]
+    settle()
     started += collect
     for p in LATER:
         reduce_step(p, 1)
@@ -507,7 +513,22 @@
     gvec[2:3, 0:512] = jnp.sum(dh2 * xhat[...], axis=0, keepdims=True)
     gvec[3:4, 0:512] = jnp.sum(dh2, axis=0, keepdims=True)
     gvec[6:7, 0:512] = jnp.sum(dy.astype(F32), axis=0, keepdims=True)
-    settle()
+    grads[SMALL][...] = jnp.zeros_like(grads[SMALL])
+
+    def laid_out(wanted):
+        result = jnp.zeros((128, 128), F32)
+        for i in wanted:
+            n = SECTIONS_OUT[i][0]
+            left = 128 * sum(m for m, _ in SECTIONS_OUT[:i])
+            cols = slice(left, left + 128 * n)
+            value = gvec[i : i + 1, 0 : 128 * n]
+            high = value.astype(BF16)
+            low = (value - high.astype(F32)).astype(BF16)
+            pick, own = pick_out[:, cols], own_out[:, cols]
+            result = result + nt(own * high, pick) + nt(own * low, pick)
+        return result
+
+    gmat[...] = laid_out((2, 3, 6, 7))
     for copy in collect:
         copy.wait_recv()
 
@@ -542,18 +563,7 @@
     gvec[5:6, 0:512] = jnp.sum(dqkv_s[:, 1024:1536].astype(F32), axis=0, keepdims=True)
     for p in FIRST:
         reduce_step(p, 2)
-    spread_out = jnp.zeros((128, 128), F32)
-    left = 0
-    for i, (n, off) in enumerate(SECTIONS_OUT):
-        cols = slice(left, left + 128 * n)
-        left += 128 * n
-        value = gvec[i : i + 1, 0 : 128 * n]
-        high = value.astype(BF16)
-        low = (value - high.astype(F32)).astype(BF16)
-        pick, own = pick_out[:, cols], own_out[:, cols]
-        spread_out = spread_out + nt(own * high, pick) + nt(own * low, pick)
-    gmat[...] = spread_out
-    grads[SMALL][...] = jnp.zeros_like(grads[SMALL])
+    gmat[...] += laid_out((0, 1, 4, 5))
 
     def small_grads(z, low, t, where, c):
         row = gmat[pl.ds(z * 32 + (low * 4 + t), 1), :]

time: 106 us -> 107 us (level)
  no operation moved by 1% of the time
where the time goes in v7:
time: 107 us; the launch traced here: 106 us
  Pallas kernels  99.3 us (93%)
  local copies, waits for them, and re-layouts  5.6 us (5%)
    pallas_call x1, Pallas kernels, run_block(): pl.pallas_call(block_kernel, out_shape=(shape((1, 128, 512), BF16), shape...  97.5 us
    concatenate x1, local copies, waits for them, and re-layouts, per_device(): jnp.concatenate([norm1_gain, norm1_bias, norm2_gain, norm2_bias, qkv_bias...  4.77 us

profile of v7, /device:TPU:1, one launch (start us, length us, event | category | flops | bytes accessed | tf_op | source)
XLA Modules:
  0.0 106.4 jit_solution(3256765814415400859)
XLA Ops:
  0.6 4.8 %concatenate.7 = bf16[48]{0:T(256)(128)(2,1)S(1)} concatenate(bf16[4]{0:T(256)(128)(2,1)} %param.19, bf16[4]{0:T(256)(128)(2,1)} %param.20, bf16[4]{0:T(256)(128)(2,1)} %param.21, bf16[4]{0:T(256)(128)(2,1)} %param.22, bf16[12]{0:T(256)(128)(2,1)} %param.24, bf16[4]{0:T(256)(128)(2,1)} %param.26, bf16[16]{0:T(256)(128)(2,1)} %param.28), dimensions={0} | concatenate | bytes 192 | tf_op jit(solution)/shard_map/concatenate | solution.py:680
  5.4 0.0 copy-start
  5.4 0.6 pad.4.small
  6.0 0.1 copy-done
  6.1 0.1 reshape.59
  6.2 0.1 reshape.60
  6.3 0.1 select_reduce_fusion
  6.4 0.6 pad_add_fusion.table
  7.0 97.5 %shard_map.263 = (bf16[1,128,512]{2,1,0:T(8,128)(2,1)}, f32[1,128,512]{2,1,0:T(8,128)}, f32[4,1536]{1,0:T(4,128)}, f32[4,512]{1,0:T(4,128)}, f32[4,2048]{1,0:T(4...) custom-call(s32[64]{0:T(128)} %pad_add_fusion.table, bf16[1,128,512]{2,1,0:T(8,128)(2,1)} %hid.1, ...), custom_call_target="tpu_custom_call" | custom-call | tf_op jit(solution)/shard_map/pallas_call | solution.py:642
  104.4 1.8 %shard_map.264 = (bf16[1,128,512]{2,1,0:T(8,128)(2,1)}, f32[1,128,512]{2,1,0:T(8,128)}, f32[4,1536]{1,0:T(4,128)}, f32[4,512]{1,0:T(4,128)}, f32[4,2048]{1,0:T(4...) custom-call(bf16[1,128,512]{2,1,0:T(8,128)(2,1)} %get-tuple-element., ...), custom_call_target="tpu_custom_call" | custom-call | tf_op jit(solution)/shard_map/pallas_call | solution.py:667
  (1 shorter events, 0.0 us)
Async XLA Ops:
  5.4 0.7 copy-start
